TPU v7x, 32 devices: a whole 2x2x4 slice. The times are simulated.
32 devices in a mesh: grp: 4 (over y, x), blk: 8 (over z, core).
Axes of the slice: x: 2, y: 2, z: 4, core: 2. Of those that a mesh axis runs over, the one named last changes fastest.
Arguments:
- residual_in: bfloat16 [256, 16384], P('grp', 'blk'), may hold values from -6 to 6
- queries: bfloat16 [256, 16384], P('grp')
- key_cache: bfloat16 [256, 8, 64, 128], P('grp', 'blk')
- value_cache: bfloat16 [256, 8, 64, 128], P('grp', 'blk'), may hold values from -6 to 6
- key_new: bfloat16 [256, 1024], P('grp'), may hold values from -6 to 6
- value_new: bfloat16 [256, 1024], P('grp'), may hold values from -6 to 6
- lengths: int32 [256], P('grp'), may hold values from 2 to 64, as said below
- ffn_gain: bfloat16 [16384], P('blk'), may hold values from 0.099609375 to 1.8984375
- gate_weight: bfloat16 [16384, 26624], P('blk', 'grp'), may hold values from -0.046875 to 0.046875
- up_weight: bfloat16 [16384, 26624], P('blk', 'grp'), may hold values from -0.046875 to 0.046875
- down_weight: bfloat16 [26624, 16384], P('grp', 'blk'), may hold values from -0.0390625 to 0.0390625
Outputs:
- layer_out: float32 [256, 16384], P('grp', 'blk')
Inputs may be any that keep to these rules, and one draw needn't show every extreme that they name: `lengths`: every sequence has at least two valid cache positions, and some sequence fills all 64.
All inputs are finite; a program needn't handle non-finite values.
Results may differ from a plain program's by a relative error of at most 0.0075.
Values may be sent and summed in bfloat16 or wider, within the bound.
No kernel may reach another device: no remote copies, remote signals or barrier semaphores. Data moves between devices by JAX's collectives and lax.ppermute only.
A program may use at most 192 MiB of HBM per device.

v0:
```python
import math

import jax
import jax.numpy as jnp
from jax import lax
from jax.sharding import PartitionSpec as P

D = 16384
HEADS = 128
KV_HEADS = 8


def partner(x, axis, distance):
    return lax.ppermute(x, axis, [(i, i ^ 1 << distance) for i in range(lax.axis_size(axis))])


def on_device(
    residual_in,
    queries,
    key_cache,
    value_cache,
    key_new,
    value_new,
    lengths,
    ffn_gain,
    gate_weight,
    up_weight,
    down_weight,
):
    cycle_size = lax.axis_size("blk")
    quarters = cycle_size // KV_HEADS
    per_kv = HEADS // KV_HEADS
    own_heads = HEADS // cycle_size
    head_size = key_cache.shape[3]
    seq_rows = residual_in.shape[0]
    positions_here = key_cache.shape[2]
    blk_index = lax.axis_index("blk")
    kv_head = blk_index // quarters
    quarter = blk_index % quarters
    score_scale = 1.0 / math.sqrt(head_size)
    group_queries = lax.dynamic_slice_in_dim(
        queries, kv_head * per_kv * head_size, per_kv * head_size, 1
    )
    group_queries = group_queries.astype(jnp.float32).reshape(seq_rows, per_kv, head_size)
    fresh_key = lax.dynamic_slice_in_dim(key_new, kv_head * head_size, head_size, 1).astype(
        jnp.float32
    )
    fresh_value = lax.dynamic_slice_in_dim(value_new, kv_head * head_size, head_size, 1).astype(
        jnp.float32
    )
    keys_here = key_cache[:, 0].astype(jnp.float32)
    values_here = value_cache[:, 0].astype(jnp.float32)
    scores = jnp.einsum("shd,spd->shp", group_queries, keys_here) * score_scale
    fresh_scores = jnp.einsum("shd,sd->sh", group_queries, fresh_key) * score_scale
    places = quarter * positions_here + jnp.arange(positions_here, dtype=jnp.int32)
    usable = (places[None, :] < lengths[:, None])[:, None, :]
    with_fresh = quarter == 0
    largest = jnp.maximum(
        jnp.max(jnp.where(usable, scores, -1e30), axis=2),
        jnp.where(with_fresh, fresh_scores, -1e30),
    )
    weights = jnp.where(usable, jnp.exp(scores - largest[..., None]), 0.0)
    fresh_weight = jnp.where(with_fresh, jnp.exp(fresh_scores - largest), 0.0)
    totals = jnp.sum(weights, axis=2) + fresh_weight
    weighted = (
        jnp.einsum("shp,spd->shd", weights, values_here)
        + fresh_weight[..., None] * fresh_value[:, None, :]
    )
    for bit_number in range(quarters.bit_length() - 1):
        peer_max, peer_total, peer_weighted = partner(
            (largest, totals, weighted), "blk", bit_number
        )
        merged = jnp.maximum(largest, peer_max)
        mine_factor = jnp.exp(largest - merged)
        peer_factor = jnp.exp(peer_max - merged)
        totals = totals * mine_factor + peer_total * peer_factor
        weighted = weighted * mine_factor[..., None] + peer_weighted * peer_factor[..., None]
        largest = merged
    attention = weighted / totals[..., None]
    own_output = lax.dynamic_slice_in_dim(attention, quarter * own_heads, own_heads, 1).reshape(
        seq_rows, own_heads * head_size
    )
    wide = residual_in.astype(jnp.float32) + own_output
    row_total = lax.psum(jnp.sum(wide * wide, axis=1), "blk")
    inverse = lax.rsqrt(row_total / D + 1e-05)
    normed = (wide * ffn_gain.astype(jnp.float32)[None, :] * inverse[:, None]).astype(jnp.bfloat16)
    piece = lax.all_gather(normed, "grp", axis=0, tiled=True)
    gate_part = jnp.dot(piece, gate_weight, preferred_element_type=jnp.float32)
    up_part = jnp.dot(piece, up_weight, preferred_element_type=jnp.float32)
    partial_sums = jnp.stack([gate_part, up_part], axis=1)
    summed = lax.psum(partial_sums, "blk")
    hidden = (jax.nn.silu(summed[:, 0]) * summed[:, 1]).astype(jnp.bfloat16)
    down_terms = jnp.dot(hidden, down_weight, preferred_element_type=jnp.float32)
    returned = lax.psum_scatter(down_terms, "grp", scatter_dimension=0, tiled=True)
    return wide + returned


def solution(mesh):
    in_specs = (
        P("grp", "blk"),
        P("grp", None),
        P("grp", "blk", None, None),
        P("grp", "blk", None, None),
        P("grp", None),
        P("grp", None),
        P("grp"),
        P("blk"),
        P("blk", "grp"),
        P("blk", "grp"),
        P("grp", "blk"),
    )
    out_specs = P("grp", "blk")
    return jax.shard_map(
        on_device, mesh=mesh, in_specs=in_specs, out_specs=out_specs, check_vma=False
    )
```

profile of v0, /device:TPU:0, one launch (start us, length us, event | category | flops | bytes accessed | tf_op | source)
XLA Modules:
  0.0 440.9 jit_solution(486423170506219050)
XLA Ops:
  6.5 0.0 copy-start
  6.5 0.0 copy-start.2
  6.5 0.0 all-gather.2.cloned.1.call-start
  6.5 0.9 iota_compare_fusion
  7.4 0.7 convert_element_type.21
  8.1 0.7 dynamic-slice_bitcast_fusion.1
  8.8 0.7 dynamic-slice_convert_fusion
  9.6 0.0 copy-done
  9.6 0.2 fusion.13
  9.9 2.0 select_reduce_fusion
  11.9 0.4 fusion.8
  12.3 1.7 fusion.5
  14.0 0.0 copy-done.2
  14.0 0.3 multiply_reduce_fusion
  14.2 18.1 %psum.14 = f32[64]{0:T(128)S(1)} all-reduce(f32[64]{0:T(128)S(1)} %multiply_reduce_fusion), channel_id=1, replica_groups=mesh['grp'=4,'blk'=8] {'blk'}, use_global_device_ids=true, to_apply=%region_3.4 | all-reduce | flops 64 | bytes 512 | tf_op jit(solution)/shard_map/psum | solution.py:84
  32.3 0.9 multiply_convert_fusion
  33.2 0.0 all-gather.2.cloned.1.call-update
  33.3 0.0 all-reduce.2.cloned.1.call-start
  33.3 24.9 %all-gather.2.cloned.1.call-done = bf16[256,2048]{1,0:T(8,128)(2,1)} async-done(((bf16[64,2048]{1,0:T(8,128)(2,1)}), bf16[256,2048]{1,0:T(8,128)(2,1)}) %all-gather.2.cloned.1.call-update) | async-done | bytes 1048592 | tf_op jit(solution)/shard_map/all_gather | solution.py:87
  58.3 0.0 copy-start.3
  58.3 18.1 %convolution_bitcast_fusion = f32[256,1,6656]{2,0,1:T(8,128)} fusion(bf16[256,2048]{1,0:T(8,128)(2,1)} %all-gather.2.cloned.1.call-done, bf16[2048,6656]{1,0:T(8,128)(2,1)} %param.20), kind=kOutput, calls=%fused_computation.1 | convolution fusion | flops 6979321856 | bytes 35127296 | tf_op jit(solution)/shard_map/dot_general | solution.py:89
  76.3 0.0 copy-done.3
  76.3 15.4 %convolution_bitcast_fusion.1 = f32[256,1,6656]{2,0,1:T(8,128)} fusion(bf16[256,2048]{1,0:T(8,128)(2,1)S(1)} %copy-done.3, bf16[2048,6656]{1,0:T(8,128)(2,1)} %param.19), kind=kOutput, calls=%fused_computation.2 | convolution fusion | flops 6979321856 | bytes 35127296 | tf_op jit(solution)/shard_map/dot_general | solution.py:88
  91.7 10.6 %pad_maximum_fusion = f32[256,2,6656]{2,0,1:T(8,128)} fusion(f32[256,1,6656]{2,0,1:T(8,128)} %convolution_bitcast_fusion, f32[256,1,6656]{2,0,1:T(8,128)} %convolution_bitcast_fusion.1), kind=kLoop, calls=%fused_computation | loop fusion | flops 3407872 | bytes 27262976 | tf_op jit(solution)/shard_map/stack | solution.py:90
  102.4 0.0 all-reduce.2.cloned.1.call-update
  102.4 0.2 reduce-scatter.2.cloned.1.call-start
  102.6 274.3 %all-reduce.2.cloned.1.call-done = f32[256,2,6656]{2,0,1:T(8,128)} async-done(((f32[256,2,6656]{2,0,1:T(8,128)}), f32[256,2,6656]{2,0,1:T(8,128)}) %all-reduce.2.cloned.1.call-update) | async-done | bytes 13631504 | tf_op jit(solution)/shard_map/psum | solution.py:91
  376.9 0.0 copy-start.1
  376.9 19.8 %fusion.2 = f32[256,2048]{1,0:T(8,128)} fusion(bf16[6656,2048]{1,0:T(8,128)(2,1)} %param.21, f32[256,2,6656]{2,0,1:T(8,128)} %all-reduce.2.cloned.1.call-done), kind=kOutput, calls=%fused_computation.7 | convolution fusion | flops 6989545472 | bytes 42991616 | tf_op jit(solution)/shard_map/dot_general | solution.py:93
  396.7 0.0 reduce-scatter.2.cloned.1.call-update
  396.8 35.6 %reduce-scatter.2.cloned.1.call-done = f32[64,2048]{1,0:T(8,128)} async-done(((f32[256,2048]{1,0:T(8,128)}), f32[64,2048]{1,0:T(8,128)}) %reduce-scatter.2.cloned.1.call-update) | async-done | bytes 524304 | tf_op jit(solution)/shard_map/reduce_scatter | solution.py:94
  432.3 2.0 fusion.12
  434.4 0.0 copy-done.1
  (5 shorter events, 0.1 us)
Async XLA Ops:
  6.5 3.0 copy-start
  6.5 7.4 %copy-start.2 = (bf16[64,2048]{1,0:T(8,128)(2,1)S(1)}, bf16[64,2048]{1,0:T(8,128)(2,1)}, u32[]{:S(2)}) copy-start(bf16[64,2048]{1,0:T(8,128)(2,1)} %param.11) | copy-start | bytes 786436
  6.5 51.7 %all-gather.2.cloned.1.call-start = ((), (), s32[]{:S(2)}) async-start(), calls=%async_computation.1 | async-start | bytes 1310720 | tf_op jit(solution)/shard_map/all_gather | solution.py:87
  33.3 343.6 %all-reduce.2.cloned.1.call-start = ((), (), s32[]{:S(2)}) async-start(), calls=%async_computation.2 | async-start | bytes 27262976 | tf_op jit(solution)/shard_map/psum | solution.py:91
  58.3 18.1 %copy-start.3 = (bf16[256,2048]{1,0:T(8,128)(2,1)S(1)}, bf16[256,2048]{1,0:T(8,128)(2,1)}, u32[]{:S(2)}) copy-start(bf16[256,2048]{1,0:T(8,128)(2,1)} %all-gather.2.cloned.1.call-done) | copy-start | bytes 3145732
  102.4 329.9 %reduce-scatter.2.cloned.1.call-start = ((), (), s32[]{:S(2)}) async-start(), calls=%async_computation.3 | async-start | bytes 2621440 | tf_op jit(solution)/shard_map/reduce_scatter | solution.py:94
  376.9 57.5 %copy-start.1 = (bf16[64,16384]{1,0:T(8,128)(2,1)S(1)}, bf16[64,16384]{1,0:T(8,128)(2,1)}, u32[]{:S(2)}) copy-start(bf16[64,16384]{1,0:T(8,128)(2,1)} %param.12) | copy-start | bytes 6291460
Sparse Core Ops, SparseCore 0:
  33.4 24.8 all-gather.1
  102.5 274.3 all-reduce.1
  396.9 35.3 reduce-scatter.1
where the time goes:
time: 441 us
  waiting for transfers between devices  335 us (76%)
  matrix products  57.2 us (13%)
  blocking collectives  18.1 us (4%)
  other arithmetic  16.6 us (4%)
  between operations  13.2 us (3%)
    psum x1, waiting for transfers between devices, on_device(): summed = lax.psum(partial_sums, 'blk')  274 us
    reduce_scatter x1, waiting for transfers between devices, on_device(): lax.psum_scatter(down_terms, 'grp', scatter_dimension=0, tiled=True)  35.6 us
    all_gather x1, waiting for transfers between devices, on_device(): piece = lax.all_gather(normed, 'grp', axis=0, tiled=True)  24.9 us
    dot_general x1, matrix products, on_device(): jnp.dot(hidden, down_weight, preferred_element_type=jnp.float32)  19.8 us
    dot_general x1, matrix products, on_device(): up_part = jnp.dot(piece, up_weight, preferred_element_type=jnp.float32)  18.1 us
    psum x1, blocking collectives, on_device(): row_total = lax.psum(jnp.sum(wide * wide, axis=1), 'blk')  18.1 us
    dot_general x1, matrix products, on_device(): gate_part = jnp.dot(piece, gate_weight, preferred_element_type=jnp.float32)  15.4 us
    another operation x1, other arithmetic, on_device(): partial_sums = jnp.stack([gate_part, up_part], axis=1)  10.6 us
  transfers between devices with their start and end apart: 3, of which 3 were waited for; matrix products, arithmetic and copies ran while one was open for 0% of the time, Pallas kernels for 0%

commit v1 on v0

v1 whole, which is shorter than its diff:
```python
import functools
import math

import jax
import jax.numpy as jnp
from jax import lax
from jax.experimental import pallas as pl
from jax.experimental.pallas import tpu as pltpu
from jax.sharding import PartitionSpec as P

D = 16384
HEADS = 128
KV_HEADS = 8
UNIT = 256
CHUNKS = 4
VMEM = 48 * 1024 * 1024


def partner(x, axis, distance):
    return lax.ppermute(x, axis, [(i, i ^ distance) for i in range(lax.axis_size(axis))])


def along_line(x, step):
    chips = lax.axis_size("blk") // 2
    hops = [(step - 1, step), (chips - step, chips - step - 1)]
    return lax.ppermute(x, "blk", [(2 * a + c, 2 * b + c) for a, b in hops for c in range(2)])


def gate_up_kernel(n_blocks, place_ref, *refs):
    blocks, (gate_ref, up_ref, first_ref, second_ref, send_ref, x_ref) = (
        refs[:n_blocks],
        refs[n_blocks:],
    )
    rows = blocks[0].shape[0]
    quarter = first_ref.shape[1]

    @pl.when(pl.program_id(0) == 0)
    def _():
        for i, block in enumerate(blocks):
            x_ref[pl.ds(pl.multiple_of(place_ref[i] * rows, rows), rows), :] = block[...]

    for i, weight in enumerate((gate_ref, up_ref)):
        y = jnp.dot(x_ref[...], weight[...], preferred_element_type=jnp.float32)
        first_ref[i] = y[:quarter]
        second_ref[i] = y[quarter : 2 * quarter]
        send_ref[i] = y[2 * quarter :].astype(jnp.bfloat16)


def gate_up(place, blocks, gate_weight, up_weight, start, units):
    rows, depth = blocks[0].shape
    total = rows * len(blocks)
    quarter = total // 4
    cols = units * UNIT
    weight_spec = pl.BlockSpec((depth, UNIT), lambda i: (0, start + i))
    return pl.pallas_call(
        functools.partial(gate_up_kernel, len(blocks)),
        grid=(units,),
        in_specs=[pl.BlockSpec(memory_space=pltpu.SMEM)]
        + [pl.BlockSpec((rows, depth), lambda i: (0, 0))] * len(blocks)
        + [weight_spec, weight_spec],
        out_specs=[
            pl.BlockSpec((2, quarter, UNIT), lambda i: (0, 0, i)),
            pl.BlockSpec((2, quarter, UNIT), lambda i: (0, 0, i)),
            pl.BlockSpec((2, 2 * quarter, UNIT), lambda i: (0, 0, i)),
        ],
        out_shape=[
            jax.ShapeDtypeStruct((2, quarter, cols), jnp.float32),
            jax.ShapeDtypeStruct((2, quarter, cols), jnp.float32),
            jax.ShapeDtypeStruct((2, 2 * quarter, cols), jnp.bfloat16),
        ],
        scratch_shapes=[pltpu.VMEM((total, depth), jnp.bfloat16)],
        compiler_params=pltpu.CompilerParams(vmem_limit_bytes=VMEM),
        cost_estimate=pl.CostEstimate(
            flops=4 * total * depth * cols,
            bytes_accessed=4 * depth * cols + 2 * total * depth + 12 * total * cols,
            transcendentals=0,
        ),
    )(place, *blocks, gate_weight, up_weight)


def down_kernel(has_total, *refs):
    parts, weight_ref, rest = refs[:4], refs[4], refs[5:]
    out_ref = rest[-1]
    x = jnp.concatenate([part[...] for part in parts], axis=0)
    y = jnp.dot(x, weight_ref[...], preferred_element_type=jnp.float32)

    @pl.when(pl.program_id(0) == 0)
    def _():
        if has_total:
            out_ref[...] = rest[0][...] + y
        else:
            out_ref[...] = y

    @pl.when(pl.program_id(0) > 0)
    def _():
        out_ref[...] += y


def down(parts, weight, total, start, units):
    quarter = parts[0].shape[0]
    width = weight.shape[1]
    out = pl.BlockSpec((4 * quarter, width), lambda i: (0, 0))
    has_total = total is not None
    return pl.pallas_call(
        functools.partial(down_kernel, has_total),
        grid=(units,),
        in_specs=[pl.BlockSpec((quarter, UNIT), lambda i: (0, i))] * 4
        + [pl.BlockSpec((UNIT, width), lambda i: (start + i, 0))]
        + [out] * has_total,
        out_specs=out,
        out_shape=jax.ShapeDtypeStruct((4 * quarter, width), jnp.float32),
        input_output_aliases={5: 0} if has_total else {},
        compiler_params=pltpu.CompilerParams(vmem_limit_bytes=VMEM),
        cost_estimate=pl.CostEstimate(
            flops=8 * quarter * units * UNIT * width,
            bytes_accessed=2 * units * UNIT * width + 32 * quarter * width,
            transcendentals=0,
        ),
    )(*parts, weight, *([total] if has_total else []))


def attend(residual_in, queries, key_cache, value_cache, key_new, value_new, lengths):
    cycle_size = lax.axis_size("blk")
    quarters = cycle_size // KV_HEADS
    per_kv = HEADS // KV_HEADS
    own_heads = HEADS // cycle_size
    head_size = key_cache.shape[3]
    seq_rows = residual_in.shape[0]
    positions_here = key_cache.shape[2]
    blk_index = lax.axis_index("blk")
    kv_head = blk_index // quarters
    quarter = blk_index % quarters
    score_scale = 1.0 / math.sqrt(head_size)
    group_queries = lax.dynamic_slice_in_dim(
        queries, kv_head * per_kv * head_size, per_kv * head_size, 1
    )
    group_queries = group_queries.astype(jnp.float32).reshape(seq_rows, per_kv, head_size)
    fresh_key = lax.dynamic_slice_in_dim(key_new, kv_head * head_size, head_size, 1).astype(
        jnp.float32
    )
    fresh_value = lax.dynamic_slice_in_dim(value_new, kv_head * head_size, head_size, 1).astype(
        jnp.float32
    )
    keys_here = key_cache[:, 0].astype(jnp.float32)
    values_here = value_cache[:, 0].astype(jnp.float32)
    scores = jnp.einsum("shd,spd->shp", group_queries, keys_here) * score_scale
    fresh_scores = jnp.einsum("shd,sd->sh", group_queries, fresh_key) * score_scale
    places = quarter * positions_here + jnp.arange(positions_here, dtype=jnp.int32)
    usable = (places[None, :] < lengths[:, None])[:, None, :]
    with_fresh = quarter == 0
    largest = jnp.maximum(
        jnp.max(jnp.where(usable, scores, -1e30), axis=2),
        jnp.where(with_fresh, fresh_scores, -1e30),
    )
    weights = jnp.where(usable, jnp.exp(scores - largest[..., None]), 0.0)
    fresh_weight = jnp.where(with_fresh, jnp.exp(fresh_scores - largest), 0.0)
    totals = jnp.sum(weights, axis=2) + fresh_weight
    weighted = (
        jnp.einsum("shp,spd->shd", weights, values_here)
        + fresh_weight[..., None] * fresh_value[:, None, :]
    )
    for bit_number in range(quarters.bit_length() - 1):
        peer_max, peer_total, peer_weighted = partner(
            (largest, totals, weighted), "blk", 1 << bit_number
        )
        merged = jnp.maximum(largest, peer_max)
        mine_factor = jnp.exp(largest - merged)
        peer_factor = jnp.exp(peer_max - merged)
        totals = totals * mine_factor + peer_total * peer_factor
        weighted = weighted * mine_factor[..., None] + peer_weighted * peer_factor[..., None]
        largest = merged
    attention = weighted / totals[..., None]
    own_output = lax.dynamic_slice_in_dim(attention, quarter * own_heads, own_heads, 1).reshape(
        seq_rows, own_heads * head_size
    )
    return residual_in.astype(jnp.float32) + own_output


def on_device(
    residual_in,
    queries,
    key_cache,
    value_cache,
    key_new,
    value_new,
    lengths,
    ffn_gain,
    gate_weight,
    up_weight,
    down_weight,
):
    groups = lax.axis_size("grp")
    group = lax.axis_index("grp")
    chips = lax.axis_size("blk") // 2
    chip, core = lax.axis_index("blk") // 2, lax.axis_index("blk") % 2
    rows = residual_in.shape[0]
    per_quarter = groups // 4
    quarter = per_quarter * rows

    wide = attend(residual_in, queries, key_cache, value_cache, key_new, value_new, lengths)

    tokens = (wide * ffn_gain.astype(jnp.float32)[None, :]).astype(jnp.bfloat16)
    blocks = [tokens] + [partner(tokens, "grp", i) for i in range(1, groups)]

    squares = jnp.sum(wide * wide, axis=1)
    for bit_number in range(lax.axis_size("blk").bit_length() - 1):
        squares = squares + partner(squares, "blk", 1 << bit_number)
    squares = jnp.stack([squares] + [partner(squares, "grp", i) for i in range(1, groups)])

    lead = 2 * core + jnp.where(chip >= chips // 2, 0, 1)
    turn = group ^ (lead * per_quarter)
    place = jnp.arange(groups, dtype=jnp.int32) ^ turn
    last_rows = jnp.arange(per_quarter, dtype=jnp.int32) + per_quarter
    inverse = lax.rsqrt(squares[last_rows ^ turn].reshape(quarter) / D + 1e-05)[:, None]

    n_units = gate_weight.shape[1] // UNIT
    edges = [n_units * i // CHUNKS for i in range(CHUNKS + 1)]
    f32 = jnp.float32
    total = None
    for start, stop in zip(edges[:-1], edges[1:]):
        first, second, send = gate_up(place, blocks, gate_weight, up_weight, start, stop - start)
        other = partner(send, "blk", 1)
        first = first + other[:, :quarter].astype(f32)
        second = second + other[:, quarter:].astype(f32)
        flow = None
        for step in range(1, chips):
            own = first if step <= chips // 2 else second
            flow = own if flow is None else own + flow.astype(f32)
            flow = along_line(flow.astype(jnp.bfloat16), step)
        sums = second + flow.astype(f32)
        gate, up_part = sums[0] * inverse, sums[1] * inverse
        hidden = (jax.nn.silu(gate) * up_part).astype(jnp.bfloat16)
        halves = [hidden, None]
        for step in range(1, chips):
            hidden = along_line(hidden, step)
            half = step // (chips // 2)
            here = (chip == step) | (chip == chips - 1 - step)
            halves[half] = hidden if halves[half] is None else jnp.where(here, hidden, halves[half])
        halves = [halves[1], halves[0]]
        theirs = [partner(half, "blk", 1) for half in halves]
        total = down(halves + theirs, down_weight, total, start, stop - start)

    terms = total.reshape(groups, rows, -1)
    own = lax.dynamic_index_in_dim(terms, turn, 0, keepdims=False)
    out = wide + own
    for i in range(1, groups):
        term = lax.dynamic_index_in_dim(terms, turn ^ i, 0, keepdims=False)
        out = out + partner(term.astype(jnp.bfloat16), "grp", i).astype(f32)
    return out


def solution(mesh):
    in_specs = (
        P("grp", "blk"),
        P("grp", None),
        P("grp", "blk", None, None),
        P("grp", "blk", None, None),
        P("grp", None),
        P("grp", None),
        P("grp"),
        P("blk"),
        P("blk", "grp"),
        P("blk", "grp"),
        P("grp", "blk"),
    )
    out_specs = P("grp", "blk")
    return jax.shard_map(
        on_device, mesh=mesh, in_specs=in_specs, out_specs=out_specs, check_vma=False
    )
```

time: 441 us -> 237 us (0.54)
  waiting for transfers between devices: 335 us -> 103 us
  Pallas kernels: 0 us -> 63.7 us
  matrix products: 57.2 us -> 2.9 us
  starting transfers between devices: 0.27 us -> 53.9 us
  blocking collectives: 18.1 us -> 0 us
  between operations: 13.2 us -> 0.75 us
  other arithmetic: 16.6 us -> 7.58 us
    psum x1 -> x0, waiting for transfers between devices: 274 us -> none  [on_device(): summed = lax.psum(partial_sums, 'blk')]
    ppermute x0 -> x48, waiting for transfers between devices: none -> 103 us  [the longest x24 82.9 us: along_line(): lax.ppermute(x, 'blk', [(2 * a + c, 2 * b + c) for a, b in hops for c in...]
    pallas_call x0 -> x8, Pallas kernels: none -> 63.7 us  [the longest x4 35.3 us: gate_up(): pl.pallas_call(functools.partial(gate_up_kernel, len(blocks)), grid=(unit...]
    dot_general x6 -> x3, matrix products: 57.2 us -> 2.9 us  [the longest x1 1.96 us: attend(): scores = jnp.einsum('shd,spd->shp', group_queries, keys_here) * score_scale]
    ppermute x0 -> x48, starting transfers between devices: none -> 53.9 us  [the longest x24 32.5 us: along_line(): lax.ppermute(x, 'blk', [(2 * a + c, 2 * b + c) for a, b in hops for c in...]
    reduce_scatter x1 -> x0, waiting for transfers between devices: 35.6 us -> none  [on_device(): lax.psum_scatter(down_terms, 'grp', scatter_dimension=0, tiled=True)]
    all_gather x1 -> x0, waiting for transfers between devices: 24.9 us -> none  [on_device(): piece = lax.all_gather(normed, 'grp', axis=0, tiled=True)]
    psum x1 -> x0, blocking collectives: 18.1 us -> none  [on_device(): row_total = lax.psum(jnp.sum(wide * wide, axis=1), 'blk')]
  transfers between devices with their start and end apart: 3 -> 48, of which waited for: 3 -> 23; matrix products, arithmetic and copies ran while one was open for 0% -> 1% of each run, Pallas kernels for 0% -> 20%
where the time goes in v1:
time: 237 us; the launch traced here: 235 us
  waiting for transfers between devices  103 us (43%)
  Pallas kernels  63.7 us (27%)
  starting transfers between devices  53.9 us (23%)
  other arithmetic  7.58 us (3%)
  local copies, waits for them, and re-layouts  3.75 us (2%)
  matrix products  2.9 us (1%)
    ppermute x24, waiting for transfers between devices, along_line(): lax.ppermute(x, 'blk', [(2 * a + c, 2 * b + c) for a, b in hops for c in...  82.9 us
    pallas_call x4, Pallas kernels, gate_up(): pl.pallas_call(functools.partial(gate_up_kernel, len(blocks)), grid=(unit...  35.3 us
    ppermute x24, starting transfers between devices, along_line(): lax.ppermute(x, 'blk', [(2 * a + c, 2 * b + c) for a, b in hops for c in...  32.5 us
    pallas_call x4, Pallas kernels, down(): pl.pallas_call(functools.partial(down_kernel, has_total), grid=(units,),...  28.4 us
    ppermute x24, starting transfers between devices, partner(): lax.ppermute(x, axis, [(i, i ^ distance) for i in range(lax.axis_size(axi...  21.4 us
    ppermute x24, waiting for transfers between devices, partner(): lax.ppermute(x, axis, [(i, i ^ distance) for i in range(lax.axis_size(axi...  19.7 us
  transfers between devices with their start and end apart: 48, of which 23 were waited for; matrix products, arithmetic and copies ran while one was open for 1% of the time, Pallas kernels for 20%

profile of v1, /device:TPU:0, one launch (start us, length us, event | category | flops | bytes accessed | tf_op | source)
XLA Modules:
  0.0 235.2 jit_solution(13884033412904698157)
XLA Ops:
  0.0 0.9 iota_compare_fusion
  0.9 0.7 copy-done
  1.7 0.8 dynamic-slice_bitcast_fusion.1
  2.7 2.0 select_reduce_fusion
  5.1 0.7 dynamic-slice_convert_fusion.3
  5.9 0.7 fusion
  6.9 3.0 %collective-permute-start = (bf16[64,2048]{1,0:T(8,128)(2,1)S(1)}, bf16[64,2048]{1,0:T(8,128)(2,1)S(1)}, u32[]{:S(2)}, u32[]{:S(2)}) collective-permute-start(bf16[64,2048]{1,0:T(8,128)(2,1)S(1)} %get-tuple-element.46.refs_0_), channel_id=1, source_target_pairs={{0,8},{8,0},{16,24},{24,16},{1,9},{9,1},{17,25},{25,17},{2,10},{10... | collective-permute-start | bytes 786440 | tf_op jit(solution)/shard_map/ppermute | solution.py:20
  9.9 1.5 collective-permute-start.1
  11.4 1.1 collective-permute-done.7
  12.6 2.0 collective-permute-start.8
  14.6 1.5 collective-permute-done.8
  16.1 3.0 %collective-permute-start.9 = (f32[64]{0:T(128)S(1)}, f32[64]{0:T(128)S(1)}, u32[]{:S(2)}, u32[]{:S(2)}) collective-permute-start(f32[64]{0:T(128)S(1)} %add.165), channel_id=1, source_target_pairs={{0,4},{1,5},{2,6},{3,7},{4,0},{5,1},{6,2},{7,3},{8,12},{9,13},{10,... | collective-permute-start | bytes 776 | tf_op jit(solution)/shard_map/ppermute | solution.py:20
  19.1 1.5 collective-permute-done.9
  20.7 2.8 %collective-permute-start.12 = (f32[64]{0:T(128)S(1)}, f32[64]{0:T(128)S(1)}, u32[]{:S(2)}, u32[]{:S(2)}) collective-permute-start(f32[64]{0:T(128)S(1)} %add.166), channel_id=1, source_target_pairs={{0,24},{8,16},{16,8},{24,0},{1,25},{9,17},{17,9},{25,1},{2,26},{10... | collective-permute-start | bytes 776 | tf_op jit(solution)/shard_map/ppermute | solution.py:20
  24.0 1.2 collective-permute-done.12
  25.1 1.8 collective-permute-start.10
  27.0 1.7 collective-permute-done.10
  28.7 8.2 %shard_map.112 = (f32[2,64,1536]{2,1,0:T(8,128)S(1)}, f32[2,64,1536]{2,1,0:T(8,128)S(1)}, bf16[2,128,1536]{2,1,0:T(8,128)(2,1)S(1)}) custom-call(s32[4]{0:T(128)S(1)} %iota_xor_fusion.place_ref, bf16[64,2048]{1,0:T(8,128)(2,1)S(1)} %get-tuple-element.46.refs_0_, bf16[64,2048]{1,0:T(8,128)(2,1)S(1)} %collective-permute-done.refs_1_, ...), custom_call_target="tpu_custom_call" | custom-call | flops 3221225472 | bytes 18350080 | tf_op jit(solution)/shard_map/pallas_call | solution.py:55
  37.0 9.5 %shard_map.111 = (f32[2,64,1792]{2,1,0:T(8,128)S(1)}, f32[2,64,1792]{2,1,0:T(8,128)S(1)}, bf16[2,128,1792]{2,1,0:T(8,128)(2,1)S(1)}) custom-call(s32[4]{0:T(128)S(1)} %iota_xor_fusion.place_ref, bf16[64,2048]{1,0:T(8,128)(2,1)S(1)} %get-tuple-element.46.refs_0_, bf16[64,2048]{1,0:T(8,128)(2,1)S(1)} %collective-permute-done.refs_1_, ...), custom_call_target="tpu_custom_call" | custom-call | flops 3758096384 | bytes 21233664 | tf_op jit(solution)/shard_map/pallas_call | solution.py:55
  47.0 8.1 %shard_map.110 = (f32[2,64,1536]{2,1,0:T(8,128)S(1)}, f32[2,64,1536]{2,1,0:T(8,128)S(1)}, bf16[2,128,1536]{2,1,0:T(8,128)(2,1)S(1)}) custom-call(s32[4]{0:T(128)S(1)} %iota_xor_fusion.place_ref, bf16[64,2048]{1,0:T(8,128)(2,1)S(1)} %get-tuple-element.46.refs_0_, bf16[64,2048]{1,0:T(8,128)(2,1)S(1)} %collective-permute-done.refs_1_, ...), custom_call_target="tpu_custom_call" | custom-call | flops 3221225472 | bytes 18350080 | tf_op jit(solution)/shard_map/pallas_call | solution.py:55
  55.3 9.5 %shard_map.109 = (f32[2,64,1792]{2,1,0:T(8,128)S(1)}, f32[2,64,1792]{2,1,0:T(8,128)S(1)}, bf16[2,128,1792]{2,1,0:T(8,128)(2,1)S(1)}) custom-call(s32[4]{0:T(128)S(1)} %iota_xor_fusion.place_ref, bf16[64,2048]{1,0:T(8,128)(2,1)S(1)} %get-tuple-element.46.refs_0_, bf16[64,2048]{1,0:T(8,128)(2,1)S(1)} %collective-permute-done.refs_1_, ...), custom_call_target="tpu_custom_call" | custom-call | flops 3758096384 | bytes 21233664 | tf_op jit(solution)/shard_map/pallas_call | solution.py:55
  65.3 3.8 %collective-permute-start.37 = (bf16[2,64,1536]{2,1,0:T(8,128)(2,1)S(1)}, bf16[2,64,1536]{2,1,0:T(8,128)(2,1)S(1)}, u32[]{:S(2)}, u32[]{:S(2)}) collective-permute-start(bf16[2,64,1536]{2,1,0:T(8,128)(2,1)S(1)} %fusion.6), channel_id=1, source_target_pairs={{0,2},{1,3},{6,4},{7,5},{8,10},{9,11},{14,12},{15,13},{16,18},{17,... | collective-permute-start | bytes 1179656 | tf_op jit(solution)/shard_map/ppermute | solution.py:26
  69.3 1.3 collective-permute-start.19
  70.7 1.3 collective-permute-start.28
  72.1 1.3 collective-permute-start.4
  73.5 5.2 %collective-permute-done.37 = bf16[2,64,1536]{2,1,0:T(8,128)(2,1)S(1)} collective-permute-done((bf16[2,64,1536]{2,1,0:T(8,128)(2,1)S(1)}, bf16[2,64,1536]{2,1,0:T(8,128)(2,1)S(1)}, u32[]{:S(2)}, u32[]{:S(2)}) %collective-permute-start.37) | collective-permute-done | bytes 393248 | tf_op jit(solution)/shard_map/ppermute | solution.py:26
  78.8 0.7 collective-permute-start.38
  79.5 7.6 %collective-permute-done.19 = bf16[2,64,1536]{2,1,0:T(8,128)(2,1)S(1)} collective-permute-done((bf16[2,64,1536]{2,1,0:T(8,128)(2,1)S(1)}, bf16[2,64,1536]{2,1,0:T(8,128)(2,1)S(1)}, u32[]{:S(2)}, u32[]{:S(2)}) %collective-permute-start.19) | collective-permute-done | bytes 393248 | tf_op jit(solution)/shard_map/ppermute | solution.py:26
  87.9 9.0 %collective-permute-done.28 = bf16[2,64,1792]{2,1,0:T(8,128)(2,1)S(1)} collective-permute-done((bf16[2,64,1792]{2,1,0:T(8,128)(2,1)S(1)}, bf16[2,64,1792]{2,1,0:T(8,128)(2,1)S(1)}, u32[]{:S(2)}, u32[]{:S(2)}) %collective-permute-start.28) | collective-permute-done | bytes 458784 | tf_op jit(solution)/shard_map/ppermute | solution.py:26
  97.0 0.7 collective-permute-start.29
  97.7 8.1 %collective-permute-done.4 = bf16[2,64,1792]{2,1,0:T(8,128)(2,1)S(1)} collective-permute-done((bf16[2,64,1792]{2,1,0:T(8,128)(2,1)S(1)}, bf16[2,64,1792]{2,1,0:T(8,128)(2,1)S(1)}, u32[]{:S(2)}, u32[]{:S(2)}) %collective-permute-start.4) | collective-permute-done | bytes 458784 | tf_op jit(solution)/shard_map/ppermute | solution.py:26
  106.0 0.7 collective-permute-start.5
  106.8 1.3 collective-permute-start.39
  108.3 1.3 collective-permute-start.21
  109.7 1.3 collective-permute-start.30
  111.0 12.4 %collective-permute-done.39 = bf16[2,64,1536]{2,1,0:T(8,128)(2,1)S(1)} collective-permute-done((bf16[2,64,1536]{2,1,0:T(8,128)(2,1)S(1)}, bf16[2,64,1536]{2,1,0:T(8,128)(2,1)S(1)}, u32[]{:S(2)}, u32[]{:S(2)}) %collective-permute-start.39) | collective-permute-done | bytes 393248 | tf_op jit(solution)/shard_map/ppermute | solution.py:26
  123.5 8.3 %collective-permute-done.21 = bf16[2,64,1536]{2,1,0:T(8,128)(2,1)S(1)} collective-permute-done((bf16[2,64,1536]{2,1,0:T(8,128)(2,1)S(1)}, bf16[2,64,1536]{2,1,0:T(8,128)(2,1)S(1)}, u32[]{:S(2)}, u32[]{:S(2)}) %collective-permute-start.21) | collective-permute-done | bytes 393248 | tf_op jit(solution)/shard_map/ppermute | solution.py:26
  132.3 1.5 collective-permute-start.22
  133.9 1.3 collective-permute-start.6
  135.2 4.6 %collective-permute-start.40 = (bf16[64,1536]{1,0:T(8,128)(2,1)S(1)}, bf16[64,1536]{1,0:T(8,128)(2,1)S(1)}, u32[]{:S(2)}, u32[]{:S(2)}) collective-permute-start(bf16[64,1536]{1,0:T(8,128)(2,1)S(1)} %get-tuple-element.47), channel_id=1, source_target_pairs={{0,2},{1,3},{6,4},{7,5},{8,10},{9,11},{14,12},{15,13},{16,18},{17,... | collective-permute-start | bytes 589832 | tf_op jit(solution)/shard_map/ppermute | solution.py:26
  140.6 2.4 %collective-permute-done.40 = bf16[64,1536]{1,0:T(8,128)(2,1)S(1)} collective-permute-done((bf16[64,1536]{1,0:T(8,128)(2,1)S(1)}, bf16[64,1536]{1,0:T(8,128)(2,1)S(1)}, u32[]{:S(2)}, u32[]{:S(2)}) %collective-permute-start.40) | collective-permute-done | bytes 196640 | tf_op jit(solution)/shard_map/ppermute | solution.py:26
  143.8 5.9 %collective-permute-done.6 = bf16[2,64,1792]{2,1,0:T(8,128)(2,1)S(1)} collective-permute-done((bf16[2,64,1792]{2,1,0:T(8,128)(2,1)S(1)}, bf16[2,64,1792]{2,1,0:T(8,128)(2,1)S(1)}, u32[]{:S(2)}, u32[]{:S(2)}) %collective-permute-start.6) | collective-permute-done | bytes 458784 | tf_op jit(solution)/shard_map/ppermute | solution.py:26
  150.1 1.5 collective-permute-start.13
  151.7 1.3 collective-permute-start.31
  153.0 1.3 collective-permute-start.24
  154.3 2.0 collective-permute-done.13
  156.3 1.3 collective-permute-start.42
  157.6 2.4 %collective-permute-done.31 = bf16[64,1792]{1,0:T(8,128)(2,1)S(1)} collective-permute-done((bf16[64,1792]{1,0:T(8,128)(2,1)S(1)}, bf16[64,1792]{1,0:T(8,128)(2,1)S(1)}, u32[]{:S(2)}, u32[]{:S(2)}) %collective-permute-start.31) | collective-permute-done | bytes 229408 | tf_op jit(solution)/shard_map/ppermute | solution.py:26
  160.7 5.7 %collective-permute-done.42 = bf16[64,1536]{1,0:T(8,128)(2,1)S(1)} collective-permute-done((bf16[64,1536]{1,0:T(8,128)(2,1)S(1)}, bf16[64,1536]{1,0:T(8,128)(2,1)S(1)}, u32[]{:S(2)}, u32[]{:S(2)}) %collective-permute-start.42) | collective-permute-done | bytes 196640 | tf_op jit(solution)/shard_map/ppermute | solution.py:26
  167.2 1.3 collective-permute-start.33
  169.2 6.4 %shard_map.113.refs_5_ = f32[256,2048]{1,0:T(8,128)S(1)} custom-call(bf16[64,1536]{1,0:T(8,128)(2,1)S(1)} %broadcast_select_fusion.6.refs_0_, bf16[64,1536]{1,0:T(8,128)(2,1)S(1)} %broadcast_select_fusion.4.refs_1_, bf16[64,1536]{1,0:T(8,128)(2,1)S(1)} %collective-permute-done.43.refs_2_, bf16[64,1536]{1,0:T(8,128)(2,1)S(1)} %collective-permute-done.44.refs_3_, ...), custom_call_target="tpu_custom_call" | custom-call | flops 1610612736 | bytes 10485760 | tf_op jit(solution)/shard_map/pallas_call | solution.py:104
  176.1 6.1 %collective-permute-done.33 = bf16[64,1792]{1,0:T(8,128)(2,1)S(1)} collective-permute-done((bf16[64,1792]{1,0:T(8,128)(2,1)S(1)}, bf16[64,1792]{1,0:T(8,128)(2,1)S(1)}, u32[]{:S(2)}, u32[]{:S(2)}) %collective-permute-start.33) | collective-permute-done | bytes 229408 | tf_op jit(solution)/shard_map/ppermute | solution.py:26
  182.2 1.5 collective-permute-start.15
  183.7 8.0 %collective-permute-done.15 = bf16[64,1792]{1,0:T(8,128)(2,1)S(1)} collective-permute-done((bf16[64,1792]{1,0:T(8,128)(2,1)S(1)}, bf16[64,1792]{1,0:T(8,128)(2,1)S(1)}, u32[]{:S(2)}, u32[]{:S(2)}) %collective-permute-start.15) | collective-permute-done | bytes 229408 | tf_op jit(solution)/shard_map/ppermute | solution.py:26
  192.3 0.9 collective-permute-done.34.refs_2_
  193.1 7.7 %shard_map.114.refs_5_ = f32[256,2048]{1,0:T(8,128)S(1)} custom-call(bf16[64,1792]{1,0:T(8,128)(2,1)S(1)} %broadcast_select_fusion.2.refs_0_, bf16[64,1792]{1,0:T(8,128)(2,1)S(1)} %broadcast_select_fusion.refs_1_, bf16[64,1792]{1,0:T(8,128)(2,1)S(1)} %collective-permute-done.34.refs_2_, ...), custom_call_target="tpu_custom_call", output_to_operand_aliasing={{}: (5, {})} | custom-call | flops 1879048192 | bytes 11534336 | tf_op jit(solution)/shard_map/pallas_call | solution.py:104
  200.9 6.6 %shard_map.115.refs_5_ = f32[256,2048]{1,0:T(8,128)S(1)} custom-call(bf16[64,1536]{1,0:T(8,128)(2,1)S(1)} %broadcast_select_fusion.7.refs_0_, bf16[64,1536]{1,0:T(8,128)(2,1)S(1)} %broadcast_select_fusion.5.refs_1_, bf16[64,1536]{1,0:T(8,128)(2,1)S(1)} %collective-permute-done.25.refs_2_, ...), custom_call_target="tpu_custom_call", output_to_operand_aliasing={{}: (5, {})} | custom-call | flops 1610612736 | bytes 10485760 | tf_op jit(solution)/shard_map/pallas_call | solution.py:104
  207.5 7.7 %shard_map.116 = f32[256,2048]{1,0:T(8,128)S(1)} custom-call(bf16[64,1792]{1,0:T(8,128)(2,1)S(1)} %broadcast_select_fusion.3.refs_0_, bf16[64,1792]{1,0:T(8,128)(2,1)S(1)} %broadcast_select_fusion.1.refs_1_, bf16[64,1792]{1,0:T(8,128)(2,1)S(1)} %collective-permute-done.16.refs_2_, ...), custom_call_target="tpu_custom_call", output_to_operand_aliasing={{}: (5, {})} | custom-call | flops 1879048192 | bytes 11534336 | tf_op jit(solution)/shard_map/pallas_call | solution.py:104
  215.3 1.3 copy-done.2
  216.6 0.8 fusion.27
  217.4 2.4 %collective-permute-start.47 = (bf16[64,2048]{1,0:T(8,128)(2,1)}, bf16[64,2048]{1,0:T(8,128)(2,1)}, u32[]{:S(2)}, u32[]{:S(2)}) collective-permute-start(bf16[64,2048]{1,0:T(8,128)(2,1)} %get-tuple-element.43), channel_id=1, source_target_pairs={{0,24},{8,16},{16,8},{24,0},{1,25},{9,17},{17,9},{25,1},{2,26},{10... | collective-permute-start | bytes 786440 | tf_op jit(solution)/shard_map/ppermute | solution.py:20
  220.9 6.9 %collective-permute-done.47 = bf16[64,2048]{1,0:T(8,128)(2,1)} collective-permute-done((bf16[64,2048]{1,0:T(8,128)(2,1)}, bf16[64,2048]{1,0:T(8,128)(2,1)}, u32[]{:S(2)}, u32[]{:S(2)}) %collective-permute-start.47) | collective-permute-done | bytes 262176 | tf_op jit(solution)/shard_map/ppermute | solution.py:20
  227.8 4.8 %collective-permute-done.46 = bf16[64,2048]{1,0:T(8,128)(2,1)} collective-permute-done((bf16[64,2048]{1,0:T(8,128)(2,1)S(1)}, bf16[64,2048]{1,0:T(8,128)(2,1)}, u32[]{:S(2)}, u32[]{:S(2)}) %collective-permute-start.46) | collective-permute-done | bytes 262176 | tf_op jit(solution)/shard_map/ppermute | solution.py:20
  232.7 2.5 %fusion.9 = f32[64,2048]{1,0:T(8,128)} fusion(bf16[64,2048]{1,0:T(8,128)(2,1)} %collective-permute-done.47, bf16[64,2048]{1,0:T(8,128)(2,1)} %collective-permute-done.46, bf16[64,2048]{1,0:T(8,128)(2,1)} %collective-permute-done.45, f32[4,64,2048]{2,1,0:T(8,128)} %bitcast.106, s32[]{:T(128)S(6)} %select_n.119, f32[8,8,16,128]{3,2,1,0:T(8,128)S(1)} %bitcast.108, ...), kind=kLoop, calls=%fused_computation.33 | loop fusion | flops 1179648 | bytes 2621444 | tf_op jit(solution)/shard_map/add | solution.py:248
  (101 shorter events, 12.1 us)
Async XLA Ops:
  0.0 1.6 copy-start
  1.6 4.3 %copy-start.5 = (bf16[2048]{0:T(1024)(128)(2,1)S(1)}, bf16[2048]{0:T(1024)(128)(2,1)}, u32[]{:S(2)}) copy-start(bf16[2048]{0:T(1024)(128)(2,1)} %param.18) | copy-start | bytes 12292
  1.6 4.2 %copy-start.6 = (bf16[64,1,64,128]{3,2,1,0:T(8,128)(2,1)S(1)}, bf16[64,1,64,128]{3,2,1,0:T(8,128)(2,1)}, u32[]{:S(2)}) copy-start(bf16[64,1,64,128]{3,2,1,0:T(8,128)(2,1)} %param.14) | copy-start | bytes 3145732
  4.7 1.9 copy-start.3
  6.9 21.8 %collective-permute-start = (bf16[64,2048]{1,0:T(8,128)(2,1)S(1)}, bf16[64,2048]{1,0:T(8,128)(2,1)S(1)}, u32[]{:S(2)}, u32[]{:S(2)}) collective-permute-start(bf16[64,2048]{1,0:T(8,128)(2,1)S(1)} %get-tuple-element.46.refs_0_), channel_id=1, source_target_pairs={{0,8},{8,0},{16,24},{24,16},{1,9},{9,1},{17,25},{25,17},{2,10},{10... | collective-permute-start | bytes 786440 | tf_op jit(solution)/shard_map/ppermute | solution.py:20
  9.9 18.8 %collective-permute-start.1 = (bf16[64,2048]{1,0:T(8,128)(2,1)S(1)}, bf16[64,2048]{1,0:T(8,128)(2,1)S(1)}, u32[]{:S(2)}, u32[]{:S(2)}) collective-permute-start(bf16[64,2048]{1,0:T(8,128)(2,1)S(1)} %get-tuple-element.46.refs_0_), channel_id=1, source_target_pairs={{0,16},{8,24},{16,0},{24,8},{1,17},{9,25},{17,1},{25,9},{2,18},{10... | collective-permute-start | bytes 786440 | tf_op jit(solution)/shard_map/ppermute | solution.py:20
  11.4 17.3 %collective-permute-start.2 = (bf16[64,2048]{1,0:T(8,128)(2,1)S(1)}, bf16[64,2048]{1,0:T(8,128)(2,1)S(1)}, u32[]{:S(2)}, u32[]{:S(2)}) collective-permute-start(bf16[64,2048]{1,0:T(8,128)(2,1)S(1)} %get-tuple-element.46.refs_0_), channel_id=1, source_target_pairs={{0,24},{8,16},{16,8},{24,0},{1,25},{9,17},{17,9},{25,1},{2,26},{10... | collective-permute-start | bytes 786440 | tf_op jit(solution)/shard_map/ppermute | solution.py:20
  11.4 1.1 collective-permute-start.7
  12.6 3.6 %collective-permute-start.8 = (f32[64]{0:T(128)S(1)}, f32[64]{0:T(128)S(1)}, u32[]{:S(2)}, u32[]{:S(2)}) collective-permute-start(f32[64]{0:T(128)S(1)} %add.164), channel_id=1, source_target_pairs={{0,2},{1,3},{2,0},{3,1},{4,6},{5,7},{6,4},{7,5},{8,10},{9,11},{10,... | collective-permute-start | bytes 776 | tf_op jit(solution)/shard_map/ppermute | solution.py:20
  16.1 4.6 %collective-permute-start.9 = (f32[64]{0:T(128)S(1)}, f32[64]{0:T(128)S(1)}, u32[]{:S(2)}, u32[]{:S(2)}) collective-permute-start(f32[64]{0:T(128)S(1)} %add.165), channel_id=1, source_target_pairs={{0,4},{1,5},{2,6},{3,7},{4,0},{5,1},{6,2},{7,3},{8,12},{9,13},{10,... | collective-permute-start | bytes 776 | tf_op jit(solution)/shard_map/ppermute | solution.py:20
  20.7 4.4 %collective-permute-start.12 = (f32[64]{0:T(128)S(1)}, f32[64]{0:T(128)S(1)}, u32[]{:S(2)}, u32[]{:S(2)}) collective-permute-start(f32[64]{0:T(128)S(1)} %add.166), channel_id=1, source_target_pairs={{0,24},{8,16},{16,8},{24,0},{1,25},{9,17},{17,9},{25,1},{2,26},{10... | collective-permute-start | bytes 776 | tf_op jit(solution)/shard_map/ppermute | solution.py:20
  23.5 3.5 %collective-permute-start.11 = (f32[64]{0:T(128)S(1)}, f32[64]{0:T(128)S(1)}, u32[]{:S(2)}, u32[]{:S(2)}) collective-permute-start(f32[64]{0:T(128)S(1)} %add.166), channel_id=1, source_target_pairs={{0,16},{8,24},{16,0},{24,8},{1,17},{9,25},{17,1},{25,9},{2,18},{10... | collective-permute-start | bytes 776 | tf_op jit(solution)/shard_map/ppermute | solution.py:20
  25.1 3.5 %collective-permute-start.10 = (f32[64]{0:T(128)S(1)}, f32[64]{0:T(128)S(1)}, u32[]{:S(2)}, u32[]{:S(2)}) collective-permute-start(f32[64]{0:T(128)S(1)} %add.166), channel_id=1, source_target_pairs={{0,8},{8,0},{16,24},{24,16},{1,9},{9,1},{17,25},{25,17},{2,10},{10... | collective-permute-start | bytes 776 | tf_op jit(solution)/shard_map/ppermute | solution.py:20
  36.9 28.4 %collective-permute-start.36 = (bf16[2,128,1536]{2,1,0:T(8,128)(2,1)S(1)}, bf16[2,128,1536]{2,1,0:T(8,128)(2,1)S(1)}, u32[]{:S(2)}, u32[]{:S(2)}) collective-permute-start(bf16[2,128,1536]{2,1,0:T(8,128)(2,1)S(1)} %get-tuple-element.27), channel_id=1, source_target_pairs={{0,1},{1,0},{2,3},{3,2},{4,5},{5,4},{6,7},{7,6},{8,9},{9,8},{10,11... | collective-permute-start | bytes 2359304 | tf_op jit(solution)/shard_map/ppermute | solution.py:20
  46.5 24.1 %collective-permute-start.27 = (bf16[2,128,1792]{2,1,0:T(8,128)(2,1)S(1)}, bf16[2,128,1792]{2,1,0:T(8,128)(2,1)S(1)}, u32[]{:S(2)}, u32[]{:S(2)}) collective-permute-start(bf16[2,128,1792]{2,1,0:T(8,128)(2,1)S(1)} %get-tuple-element.24), channel_id=1, source_target_pairs={{0,1},{1,0},{2,3},{3,2},{4,5},{5,4},{6,7},{7,6},{8,9},{9,8},{10,11... | collective-permute-start | bytes 2752520 | tf_op jit(solution)/shard_map/ppermute | solution.py:20
  55.2 14.0 %collective-permute-start.18 = (bf16[2,128,1536]{2,1,0:T(8,128)(2,1)S(1)}, bf16[2,128,1536]{2,1,0:T(8,128)(2,1)S(1)}, u32[]{:S(2)}, u32[]{:S(2)}) collective-permute-start(bf16[2,128,1536]{2,1,0:T(8,128)(2,1)S(1)} %get-tuple-element.21), channel_id=1, source_target_pairs={{0,1},{1,0},{2,3},{3,2},{4,5},{5,4},{6,7},{7,6},{8,9},{9,8},{10,11... | collective-permute-start | bytes 2359304 | tf_op jit(solution)/shard_map/ppermute | solution.py:20
  64.7 7.3 %collective-permute-start.3 = (bf16[2,128,1792]{2,1,0:T(8,128)(2,1)S(1)}, bf16[2,128,1792]{2,1,0:T(8,128)(2,1)S(1)}, u32[]{:S(2)}, u32[]{:S(2)}) collective-permute-start(bf16[2,128,1792]{2,1,0:T(8,128)(2,1)S(1)} %get-tuple-element.18), channel_id=1, source_target_pairs={{0,1},{1,0},{2,3},{3,2},{4,5},{5,4},{6,7},{7,6},{8,9},{9,8},{10,11... | collective-permute-start | bytes 2752520 | tf_op jit(solution)/shard_map/ppermute | solution.py:20
  65.3 13.3 %collective-permute-start.37 = (bf16[2,64,1536]{2,1,0:T(8,128)(2,1)S(1)}, bf16[2,64,1536]{2,1,0:T(8,128)(2,1)S(1)}, u32[]{:S(2)}, u32[]{:S(2)}) collective-permute-start(bf16[2,64,1536]{2,1,0:T(8,128)(2,1)S(1)} %fusion.6), channel_id=1, source_target_pairs={{0,2},{1,3},{6,4},{7,5},{8,10},{9,11},{14,12},{15,13},{16,18},{17,... | collective-permute-start | bytes 1179656 | tf_op jit(solution)/shard_map/ppermute | solution.py:26
  69.3 17.8 %collective-permute-start.19 = (bf16[2,64,1536]{2,1,0:T(8,128)(2,1)S(1)}, bf16[2,64,1536]{2,1,0:T(8,128)(2,1)S(1)}, u32[]{:S(2)}, u32[]{:S(2)}) collective-permute-start(bf16[2,64,1536]{2,1,0:T(8,128)(2,1)S(1)} %fusion.5), channel_id=1, source_target_pairs={{0,2},{1,3},{6,4},{7,5},{8,10},{9,11},{14,12},{15,13},{16,18},{17,... | collective-permute-start | bytes 1179656 | tf_op jit(solution)/shard_map/ppermute | solution.py:26
  70.7 26.2 %collective-permute-start.28 = (bf16[2,64,1792]{2,1,0:T(8,128)(2,1)S(1)}, bf16[2,64,1792]{2,1,0:T(8,128)(2,1)S(1)}, u32[]{:S(2)}, u32[]{:S(2)}) collective-permute-start(bf16[2,64,1792]{2,1,0:T(8,128)(2,1)S(1)} %fusion.4), channel_id=1, source_target_pairs={{0,2},{1,3},{6,4},{7,5},{8,10},{9,11},{14,12},{15,13},{16,18},{17,... | collective-permute-start | bytes 1376264 | tf_op jit(solution)/shard_map/ppermute | solution.py:26
  72.1 33.7 %collective-permute-start.4 = (bf16[2,64,1792]{2,1,0:T(8,128)(2,1)S(1)}, bf16[2,64,1792]{2,1,0:T(8,128)(2,1)S(1)}, u32[]{:S(2)}, u32[]{:S(2)}) collective-permute-start(bf16[2,64,1792]{2,1,0:T(8,128)(2,1)S(1)} %fusion.3), channel_id=1, source_target_pairs={{0,2},{1,3},{6,4},{7,5},{8,10},{9,11},{14,12},{15,13},{16,18},{17,... | collective-permute-start | bytes 1376264 | tf_op jit(solution)/shard_map/ppermute | solution.py:26
  78.8 27.9 %collective-permute-start.38 = (bf16[2,64,1536]{2,1,0:T(8,128)(2,1)S(1)}, bf16[2,64,1536]{2,1,0:T(8,128)(2,1)S(1)}, u32[]{:S(2)}, u32[]{:S(2)}) collective-permute-start(bf16[2,64,1536]{2,1,0:T(8,128)(2,1)S(1)} %add_convert_fusion.5), channel_id=1, source_target_pairs={{2,4},{3,5},{4,2},{5,3},{10,12},{11,13},{12,10},{13,11},{18,20},{1... | collective-permute-start | bytes 1179656 | tf_op jit(solution)/shard_map/ppermute | solution.py:26
  87.2 20.9 %collective-permute-start.20 = (bf16[2,64,1536]{2,1,0:T(8,128)(2,1)S(1)}, bf16[2,64,1536]{2,1,0:T(8,128)(2,1)S(1)}, u32[]{:S(2)}, u32[]{:S(2)}) collective-permute-start(bf16[2,64,1536]{2,1,0:T(8,128)(2,1)S(1)} %add_convert_fusion.7), channel_id=1, source_target_pairs={{2,4},{3,5},{4,2},{5,3},{10,12},{11,13},{12,10},{13,11},{18,20},{1... | collective-permute-start | bytes 1179656 | tf_op jit(solution)/shard_map/ppermute | solution.py:26
  97.0 12.5 %collective-permute-start.29 = (bf16[2,64,1792]{2,1,0:T(8,128)(2,1)S(1)}, bf16[2,64,1792]{2,1,0:T(8,128)(2,1)S(1)}, u32[]{:S(2)}, u32[]{:S(2)}) collective-permute-start(bf16[2,64,1792]{2,1,0:T(8,128)(2,1)S(1)} %add_convert_fusion.1), channel_id=1, source_target_pairs={{2,4},{3,5},{4,2},{5,3},{10,12},{11,13},{12,10},{13,11},{18,20},{1... | collective-permute-start | bytes 1376264 | tf_op jit(solution)/shard_map/ppermute | solution.py:26
  106.0 27.8 %collective-permute-start.5 = (bf16[2,64,1792]{2,1,0:T(8,128)(2,1)S(1)}, bf16[2,64,1792]{2,1,0:T(8,128)(2,1)S(1)}, u32[]{:S(2)}, u32[]{:S(2)}) collective-permute-start(bf16[2,64,1792]{2,1,0:T(8,128)(2,1)S(1)} %add_convert_fusion.3), channel_id=1, source_target_pairs={{2,4},{3,5},{4,2},{5,3},{10,12},{11,13},{12,10},{13,11},{18,20},{1... | collective-permute-start | bytes 1376264 | tf_op jit(solution)/shard_map/ppermute | solution.py:26
  106.8 16.6 %collective-permute-start.39 = (bf16[2,64,1536]{2,1,0:T(8,128)(2,1)S(1)}, bf16[2,64,1536]{2,1,0:T(8,128)(2,1)S(1)}, u32[]{:S(2)}, u32[]{:S(2)}) collective-permute-start(bf16[2,64,1536]{2,1,0:T(8,128)(2,1)S(1)} %add_convert_fusion.4), channel_id=1, source_target_pairs={{4,6},{5,7},{2,0},{3,1},{12,14},{13,15},{10,8},{11,9},{20,22},{21,... | collective-permute-start | bytes 1179656 | tf_op jit(solution)/shard_map/ppermute | solution.py:26
  108.3 23.6 %collective-permute-start.21 = (bf16[2,64,1536]{2,1,0:T(8,128)(2,1)S(1)}, bf16[2,64,1536]{2,1,0:T(8,128)(2,1)S(1)}, u32[]{:S(2)}, u32[]{:S(2)}) collective-permute-start(bf16[2,64,1536]{2,1,0:T(8,128)(2,1)S(1)} %add_convert_fusion.6), channel_id=1, source_target_pairs={{4,6},{5,7},{2,0},{3,1},{12,14},{13,15},{10,8},{11,9},{20,22},{21,... | collective-permute-start | bytes 1179656 | tf_op jit(solution)/shard_map/ppermute | solution.py:26
  109.7 33.9 %collective-permute-start.30 = (bf16[2,64,1792]{2,1,0:T(8,128)(2,1)S(1)}, bf16[2,64,1792]{2,1,0:T(8,128)(2,1)S(1)}, u32[]{:S(2)}, u32[]{:S(2)}) collective-permute-start(bf16[2,64,1792]{2,1,0:T(8,128)(2,1)S(1)} %add_convert_fusion), channel_id=1, source_target_pairs={{4,6},{5,7},{2,0},{3,1},{12,14},{13,15},{10,8},{11,9},{20,22},{21,... | collective-permute-start | bytes 1376264 | tf_op jit(solution)/shard_map/ppermute | solution.py:26
  132.3 7.5 %collective-permute-start.22 = (bf16[64,1536]{1,0:T(8,128)(2,1)S(1)}, bf16[64,1536]{1,0:T(8,128)(2,1)S(1)}, u32[]{:S(2)}, u32[]{:S(2)}) collective-permute-start(bf16[64,1536]{1,0:T(8,128)(2,1)S(1)} %get-tuple-element.48), channel_id=1, source_target_pairs={{0,2},{1,3},{6,4},{7,5},{8,10},{9,11},{14,12},{15,13},{16,18},{17,... | collective-permute-start | bytes 589832 | tf_op jit(solution)/shard_map/ppermute | solution.py:26
  133.9 15.7 %collective-permute-start.6 = (bf16[2,64,1792]{2,1,0:T(8,128)(2,1)S(1)}, bf16[2,64,1792]{2,1,0:T(8,128)(2,1)S(1)}, u32[]{:S(2)}, u32[]{:S(2)}) collective-permute-start(bf16[2,64,1792]{2,1,0:T(8,128)(2,1)S(1)} %add_convert_fusion.2), channel_id=1, source_target_pairs={{4,6},{5,7},{2,0},{3,1},{12,14},{13,15},{10,8},{11,9},{20,22},{21,... | collective-permute-start | bytes 1376264 | tf_op jit(solution)/shard_map/ppermute | solution.py:26
  135.2 7.7 %collective-permute-start.40 = (bf16[64,1536]{1,0:T(8,128)(2,1)S(1)}, bf16[64,1536]{1,0:T(8,128)(2,1)S(1)}, u32[]{:S(2)}, u32[]{:S(2)}) collective-permute-start(bf16[64,1536]{1,0:T(8,128)(2,1)S(1)} %get-tuple-element.47), channel_id=1, source_target_pairs={{0,2},{1,3},{6,4},{7,5},{8,10},{9,11},{14,12},{15,13},{16,18},{17,... | collective-permute-start | bytes 589832 | tf_op jit(solution)/shard_map/ppermute | solution.py:26
  139.8 61.0 %collective-permute-start.26 = (bf16[64,1536]{1,0:T(8,128)(2,1)S(1)}, bf16[64,1536]{1,0:T(8,128)(2,1)S(1)}, u32[]{:S(2)}, u32[]{:S(2)}) collective-permute-start(bf16[64,1536]{1,0:T(8,128)(2,1)S(1)} %broadcast_select_fusion.5.refs_1_), channel_id=1, source_target_pairs={{0,1},{1,0},{2,3},{3,2},{4,5},{5,4},{6,7},{7,6},{8,9},{9,8},{10,11... | collective-permute-start | bytes 589832 | tf_op jit(solution)/shard_map/ppermute | solution.py:20
  139.9 11.8 %collective-permute-start.23 = (bf16[64,1536]{1,0:T(8,128)(2,1)S(1)}, bf16[64,1536]{1,0:T(8,128)(2,1)S(1)}, u32[]{:S(2)}, u32[]{:S(2)}) collective-permute-start(bf16[64,1536]{1,0:T(8,128)(2,1)S(1)} %collective-permute-done.22), channel_id=1, source_target_pairs={{2,4},{3,5},{4,2},{5,3},{10,12},{11,13},{12,10},{13,11},{18,20},{1... | collective-permute-start | bytes 589832 | tf_op jit(solution)/shard_map/ppermute | solution.py:26
  143.0 10.1 %collective-permute-start.41 = (bf16[64,1536]{1,0:T(8,128)(2,1)S(1)}, bf16[64,1536]{1,0:T(8,128)(2,1)S(1)}, u32[]{:S(2)}, u32[]{:S(2)}) collective-permute-start(bf16[64,1536]{1,0:T(8,128)(2,1)S(1)} %collective-permute-done.40), channel_id=1, source_target_pairs={{2,4},{3,5},{4,2},{5,3},{10,12},{11,13},{12,10},{13,11},{18,20},{1... | collective-permute-start | bytes 589832 | tf_op jit(solution)/shard_map/ppermute | solution.py:26
  150.1 6.2 %collective-permute-start.13 = (bf16[64,1792]{1,0:T(8,128)(2,1)S(1)}, bf16[64,1792]{1,0:T(8,128)(2,1)S(1)}, u32[]{:S(2)}, u32[]{:S(2)}) collective-permute-start(bf16[64,1792]{1,0:T(8,128)(2,1)S(1)} %get-tuple-element.50), channel_id=1, source_target_pairs={{0,2},{1,3},{6,4},{7,5},{8,10},{9,11},{14,12},{15,13},{16,18},{17,... | collective-permute-start | bytes 688136 | tf_op jit(solution)/shard_map/ppermute | solution.py:26
  151.6 16.9 %collective-permute-start.44 = (bf16[64,1536]{1,0:T(8,128)(2,1)S(1)}, bf16[64,1536]{1,0:T(8,128)(2,1)S(1)}, u32[]{:S(2)}, u32[]{:S(2)}) collective-permute-start(bf16[64,1536]{1,0:T(8,128)(2,1)S(1)} %broadcast_select_fusion.4.refs_1_), channel_id=1, source_target_pairs={{0,1},{1,0},{2,3},{3,2},{4,5},{5,4},{6,7},{7,6},{8,9},{9,8},{10,11... | collective-permute-start | bytes 589832 | tf_op jit(solution)/shard_map/ppermute | solution.py:20
  151.7 8.3 %collective-permute-start.31 = (bf16[64,1792]{1,0:T(8,128)(2,1)S(1)}, bf16[64,1792]{1,0:T(8,128)(2,1)S(1)}, u32[]{:S(2)}, u32[]{:S(2)}) collective-permute-start(bf16[64,1792]{1,0:T(8,128)(2,1)S(1)} %get-tuple-element.49), channel_id=1, source_target_pairs={{0,2},{1,3},{6,4},{7,5},{8,10},{9,11},{14,12},{15,13},{16,18},{17,... | collective-permute-start | bytes 688136 | tf_op jit(solution)/shard_map/ppermute | solution.py:26
  153.0 14.1 %collective-permute-start.24 = (bf16[64,1536]{1,0:T(8,128)(2,1)S(1)}, bf16[64,1536]{1,0:T(8,128)(2,1)S(1)}, u32[]{:S(2)}, u32[]{:S(2)}) collective-permute-start(bf16[64,1536]{1,0:T(8,128)(2,1)S(1)} %collective-permute-done.23), channel_id=1, source_target_pairs={{4,6},{5,7},{2,0},{3,1},{12,14},{13,15},{10,8},{11,9},{20,22},{21,... | collective-permute-start | bytes 589832 | tf_op jit(solution)/shard_map/ppermute | solution.py:26
  156.3 10.1 %collective-permute-start.42 = (bf16[64,1536]{1,0:T(8,128)(2,1)S(1)}, bf16[64,1536]{1,0:T(8,128)(2,1)S(1)}, u32[]{:S(2)}, u32[]{:S(2)}) collective-permute-start(bf16[64,1536]{1,0:T(8,128)(2,1)S(1)} %collective-permute-done.41), channel_id=1, source_target_pairs={{4,6},{5,7},{2,0},{3,1},{12,14},{13,15},{10,8},{11,9},{20,22},{21,... | collective-permute-start | bytes 589832 | tf_op jit(solution)/shard_map/ppermute | solution.py:26
  160.0 15.6 %collective-permute-start.14 = (bf16[64,1792]{1,0:T(8,128)(2,1)S(1)}, bf16[64,1792]{1,0:T(8,128)(2,1)S(1)}, u32[]{:S(2)}, u32[]{:S(2)}) collective-permute-start(bf16[64,1792]{1,0:T(8,128)(2,1)S(1)} %collective-permute-done.13), channel_id=1, source_target_pairs={{2,4},{3,5},{4,2},{5,3},{10,12},{11,13},{12,10},{13,11},{18,20},{1... | collective-permute-start | bytes 688136 | tf_op jit(solution)/shard_map/ppermute | solution.py:26
  166.4 0.8 collective-permute-start.32
  167.1 2.0 collective-permute-start.43
  167.2 15.0 %collective-permute-start.33 = (bf16[64,1792]{1,0:T(8,128)(2,1)S(1)}, bf16[64,1792]{1,0:T(8,128)(2,1)S(1)}, u32[]{:S(2)}, u32[]{:S(2)}) collective-permute-start(bf16[64,1792]{1,0:T(8,128)(2,1)S(1)} %collective-permute-done.32), channel_id=1, source_target_pairs={{4,6},{5,7},{2,0},{3,1},{12,14},{13,15},{10,8},{11,9},{20,22},{21,... | collective-permute-start | bytes 688136 | tf_op jit(solution)/shard_map/ppermute | solution.py:26
  168.6 38.9 %collective-permute-start.17 = (bf16[64,1792]{1,0:T(8,128)(2,1)S(1)}, bf16[64,1792]{1,0:T(8,128)(2,1)S(1)}, u32[]{:S(2)}, u32[]{:S(2)}) collective-permute-start(bf16[64,1792]{1,0:T(8,128)(2,1)S(1)} %broadcast_select_fusion.1.refs_1_), channel_id=1, source_target_pairs={{0,1},{1,0},{2,3},{3,2},{4,5},{5,4},{6,7},{7,6},{8,9},{9,8},{10,11... | collective-permute-start | bytes 688136 | tf_op jit(solution)/shard_map/ppermute | solution.py:20
  169.1 22.6 %collective-permute-start.35 = (bf16[64,1792]{1,0:T(8,128)(2,1)S(1)}, bf16[64,1792]{1,0:T(8,128)(2,1)S(1)}, u32[]{:S(2)}, u32[]{:S(2)}) collective-permute-start(bf16[64,1792]{1,0:T(8,128)(2,1)S(1)} %broadcast_select_fusion.refs_1_), channel_id=1, source_target_pairs={{0,1},{1,0},{2,3},{3,2},{4,5},{5,4},{6,7},{7,6},{8,9},{9,8},{10,11... | collective-permute-start | bytes 688136 | tf_op jit(solution)/shard_map/ppermute | solution.py:20
  175.6 25.2 %collective-permute-start.25 = (bf16[64,1536]{1,0:T(8,128)(2,1)S(1)}, bf16[64,1536]{1,0:T(8,128)(2,1)S(1)}, u32[]{:S(2)}, u32[]{:S(2)}) collective-permute-start(bf16[64,1536]{1,0:T(8,128)(2,1)S(1)} %broadcast_select_fusion.7.refs_0_), channel_id=1, source_target_pairs={{0,1},{1,0},{2,3},{3,2},{4,5},{5,4},{6,7},{7,6},{8,9},{9,8},{10,11... | collective-permute-start | bytes 589832 | tf_op jit(solution)/shard_map/ppermute | solution.py:20
  182.2 9.5 %collective-permute-start.15 = (bf16[64,1792]{1,0:T(8,128)(2,1)S(1)}, bf16[64,1792]{1,0:T(8,128)(2,1)S(1)}, u32[]{:S(2)}, u32[]{:S(2)}) collective-permute-start(bf16[64,1792]{1,0:T(8,128)(2,1)S(1)} %collective-permute-done.14), channel_id=1, source_target_pairs={{4,6},{5,7},{2,0},{3,1},{12,14},{13,15},{10,8},{11,9},{20,22},{21,... | collective-permute-start | bytes 688136 | tf_op jit(solution)/shard_map/ppermute | solution.py:26
  191.6 1.5 collective-permute-start.34
  191.7 15.8 %collective-permute-start.16 = (bf16[64,1792]{1,0:T(8,128)(2,1)S(1)}, bf16[64,1792]{1,0:T(8,128)(2,1)S(1)}, u32[]{:S(2)}, u32[]{:S(2)}) collective-permute-start(bf16[64,1792]{1,0:T(8,128)(2,1)S(1)} %broadcast_select_fusion.3.refs_0_), channel_id=1, source_target_pairs={{0,1},{1,0},{2,3},{3,2},{4,5},{5,4},{6,7},{7,6},{8,9},{9,8},{10,11... | collective-permute-start | bytes 688136 | tf_op jit(solution)/shard_map/ppermute | solution.py:20
  207.5 25.2 %copy-start.4 = (bf16[64,2048]{1,0:T(8,128)(2,1)S(1)}, bf16[64,2048]{1,0:T(8,128)(2,1)}, u32[]{:S(2)}) copy-start(bf16[64,2048]{1,0:T(8,128)(2,1)} %param.11) | copy-start | bytes 786436
  215.2 1.4 copy-start.2
  215.3 19.9 %copy-start.1 = (bf16[64,16384]{1,0:T(8,128)(2,1)S(1)}, bf16[64,16384]{1,0:T(8,128)(2,1)}, u32[]{:S(2)}) copy-start(bf16[64,16384]{1,0:T(8,128)(2,1)} %param.12) | copy-start | bytes 6291460
  217.4 10.4 %collective-permute-start.47 = (bf16[64,2048]{1,0:T(8,128)(2,1)}, bf16[64,2048]{1,0:T(8,128)(2,1)}, u32[]{:S(2)}, u32[]{:S(2)}) collective-permute-start(bf16[64,2048]{1,0:T(8,128)(2,1)} %get-tuple-element.43), channel_id=1, source_target_pairs={{0,24},{8,16},{16,8},{24,0},{1,25},{9,17},{17,9},{25,1},{2,26},{10... | collective-permute-start | bytes 786440 | tf_op jit(solution)/shard_map/ppermute | solution.py:20
  219.9 12.7 %collective-permute-start.46 = (bf16[64,2048]{1,0:T(8,128)(2,1)S(1)}, bf16[64,2048]{1,0:T(8,128)(2,1)}, u32[]{:S(2)}, u32[]{:S(2)}) collective-permute-start(bf16[64,2048]{1,0:T(8,128)(2,1)S(1)} %get-tuple-element.44), channel_id=1, source_target_pairs={{0,16},{8,24},{16,0},{24,8},{1,17},{9,25},{17,1},{25,9},{2,18},{10... | collective-permute-start | bytes 786440 | tf_op jit(solution)/shard_map/ppermute | solution.py:20
  220.4 12.3 %collective-permute-start.45 = (bf16[64,2048]{1,0:T(8,128)(2,1)S(1)}, bf16[64,2048]{1,0:T(8,128)(2,1)}, u32[]{:S(2)}, u32[]{:S(2)}) collective-permute-start(bf16[64,2048]{1,0:T(8,128)(2,1)S(1)} %get-tuple-element.42), channel_id=1, source_target_pairs={{0,8},{8,0},{16,24},{24,16},{1,9},{9,1},{17,25},{25,17},{2,10},{10... | collective-permute-start | bytes 786440 | tf_op jit(solution)/shard_map/ppermute | solution.py:20

commit v2 on v1

--- a/solution.py
+++ b/solution.py
@@ -11,8 +11,7 @@
 D = 16384
 HEADS = 128
 KV_HEADS = 8
-UNIT = 256
-CHUNKS = 4
+CHUNK_UNITS = (3, 4, 3, 3)
 VMEM = 48 * 1024 * 1024
 
 
@@ -26,11 +25,11 @@
     return lax.ppermute(x, "blk", [(2 * a + c, 2 * b + c) for a, b in hops for c in range(2)])
 
 
-def gate_up_kernel(n_blocks, place_ref, *refs):
-    blocks, (gate_ref, up_ref, first_ref, second_ref, send_ref, x_ref) = (
-        refs[:n_blocks],
-        refs[n_blocks:],
-    )
+def gate_up_kernel(n_blocks, ride_at, place_ref, *refs):
+    blocks, gate_ref, up_ref = refs[:n_blocks], refs[n_blocks], refs[n_blocks + 1]
+    *_, first_ref, second_ref, send_ref, x_ref = refs if ride_at is None else refs[:-2] + refs[-1:]
+    if ride_at is not None:
+        refs[-2][...] = refs[ride_at][...]
     rows = blocks[0].shape[0]
     quarter = first_ref.shape[1]
 
@@ -46,28 +45,34 @@
         send_ref[i] = y[2 * quarter :].astype(jnp.bfloat16)
 
 
-def gate_up(place, blocks, gate_weight, up_weight, start, units):
+def gate_up(place, blocks, gate_weight, up_weight, unit, start, units, after, ride=None):
     rows, depth = blocks[0].shape
     total = rows * len(blocks)
     quarter = total // 4
-    cols = units * UNIT
-    weight_spec = pl.BlockSpec((depth, UNIT), lambda i: (0, start + i))
+    cols = units * unit
+    weight_spec = pl.BlockSpec((depth, unit), lambda i: (0, start + i))
+    rides = [] if ride is None else [ride]
+    ride_spec = [pl.BlockSpec(r.shape, lambda i: (0, 0)) for r in rides]
     return pl.pallas_call(
-        functools.partial(gate_up_kernel, len(blocks)),
+        functools.partial(gate_up_kernel, len(blocks), len(blocks) + 2 if rides else None),
         grid=(units,),
         in_specs=[pl.BlockSpec(memory_space=pltpu.SMEM)]
         + [pl.BlockSpec((rows, depth), lambda i: (0, 0))] * len(blocks)
-        + [weight_spec, weight_spec],
+        + [weight_spec, weight_spec]
+        + ride_spec
+        + [pl.BlockSpec(memory_space=pl.ANY)] * len(after),
         out_specs=[
-            pl.BlockSpec((2, quarter, UNIT), lambda i: (0, 0, i)),
-            pl.BlockSpec((2, quarter, UNIT), lambda i: (0, 0, i)),
-            pl.BlockSpec((2, 2 * quarter, UNIT), lambda i: (0, 0, i)),
-        ],
+            pl.BlockSpec((2, quarter, unit), lambda i: (0, 0, i)),
+            pl.BlockSpec((2, quarter, unit), lambda i: (0, 0, i)),
+            pl.BlockSpec((2, 2 * quarter, unit), lambda i: (0, 0, i)),
+        ]
+        + ride_spec,
         out_shape=[
             jax.ShapeDtypeStruct((2, quarter, cols), jnp.float32),
             jax.ShapeDtypeStruct((2, quarter, cols), jnp.float32),
             jax.ShapeDtypeStruct((2, 2 * quarter, cols), jnp.bfloat16),
-        ],
+        ]
+        + [jax.ShapeDtypeStruct(r.shape, r.dtype) for r in rides],
         scratch_shapes=[pltpu.VMEM((total, depth), jnp.bfloat16)],
         compiler_params=pltpu.CompilerParams(vmem_limit_bytes=VMEM),
         cost_estimate=pl.CostEstimate(
@@ -75,19 +80,47 @@
             bytes_accessed=4 * depth * cols + 2 * total * depth + 12 * total * cols,
             transcendentals=0,
         ),
-    )(place, *blocks, gate_weight, up_weight)
+    )(place, *blocks, gate_weight, up_weight, *rides, *after)
+
+
+def hidden_kernel(flow_ref, own_ref, other_ref, inverse_ref, out_ref):
+    inverse = inverse_ref[...]
+    gate, up = [
+        (own_ref[i] + other_ref[i].astype(jnp.float32) + flow_ref[i].astype(jnp.float32)) * inverse
+        for i in range(2)
+    ]
+    out_ref[...] = (gate / (1 + jnp.exp(-gate)) * up).astype(out_ref.dtype)
+
+
+def hidden_units(flow, own, other, inverse):
+    _, rows, cols = own.shape
+    tile = 256
+    return pl.pallas_call(
+        hidden_kernel,
+        grid=(cols // tile,),
+        in_specs=[
+            pl.BlockSpec((2, rows, tile), lambda i: (0, 0, i)),
+            pl.BlockSpec((2, rows, tile), lambda i: (0, 0, i)),
+            pl.BlockSpec((2, rows, tile), lambda i: (0, 1, i)),
+            pl.BlockSpec((rows, 1), lambda i: (0, 0)),
+        ],
+        out_specs=pl.BlockSpec((rows, tile), lambda i: (0, i)),
+        out_shape=jax.ShapeDtypeStruct((rows, cols), jnp.bfloat16),
+        cost_estimate=pl.CostEstimate(
+            flops=16 * rows * cols, bytes_accessed=18 * rows * cols, transcendentals=rows * cols
+        ),
+    )(flow, own, other, inverse)
 
 
 def down_kernel(has_total, *refs):
-    parts, weight_ref, rest = refs[:4], refs[4], refs[5:]
-    out_ref = rest[-1]
+    parts, weight_ref, total_ref, out_ref = refs[:4], refs[4], refs[5], refs[-1]
     x = jnp.concatenate([part[...] for part in parts], axis=0)
     y = jnp.dot(x, weight_ref[...], preferred_element_type=jnp.float32)
 
     @pl.when(pl.program_id(0) == 0)
     def _():
         if has_total:
-            out_ref[...] = rest[0][...] + y
+            out_ref[...] = total_ref[...] + y
         else:
             out_ref[...] = y
 
@@ -96,7 +129,7 @@
         out_ref[...] += y
 
 
-def down(parts, weight, total, start, units):
+def down(parts, weight, total, unit, start, units, after):
     quarter = parts[0].shape[0]
     width = weight.shape[1]
     out = pl.BlockSpec((4 * quarter, width), lambda i: (0, 0))
@@ -104,19 +137,20 @@
     return pl.pallas_call(
         functools.partial(down_kernel, has_total),
         grid=(units,),
-        in_specs=[pl.BlockSpec((quarter, UNIT), lambda i: (0, i))] * 4
-        + [pl.BlockSpec((UNIT, width), lambda i: (start + i, 0))]
-        + [out] * has_total,
+        in_specs=[pl.BlockSpec((quarter, unit), lambda i: (0, i))] * 4
+        + [pl.BlockSpec((unit, width), lambda i: (start + i, 0))]
+        + [out] * has_total
+        + [pl.BlockSpec(memory_space=pl.ANY)] * len(after),
         out_specs=out,
         out_shape=jax.ShapeDtypeStruct((4 * quarter, width), jnp.float32),
         input_output_aliases={5: 0} if has_total else {},
         compiler_params=pltpu.CompilerParams(vmem_limit_bytes=VMEM),
         cost_estimate=pl.CostEstimate(
-            flops=8 * quarter * units * UNIT * width,
-            bytes_accessed=2 * units * UNIT * width + 32 * quarter * width,
+            flops=8 * quarter * units * unit * width,
+            bytes_accessed=2 * units * unit * width + 32 * quarter * width,
             transcendentals=0,
         ),
-    )(*parts, weight, *([total] if has_total else []))
+    )(*parts, weight, *([total] if has_total else []), *after)
 
 
 def attend(residual_in, queries, key_cache, value_cache, key_new, value_new, lengths):
@@ -205,40 +239,50 @@
     squares = jnp.sum(wide * wide, axis=1)
     for bit_number in range(lax.axis_size("blk").bit_length() - 1):
         squares = squares + partner(squares, "blk", 1 << bit_number)
-    squares = jnp.stack([squares] + [partner(squares, "grp", i) for i in range(1, groups)])
 
     lead = 2 * core + jnp.where(chip >= chips // 2, 0, 1)
     turn = group ^ (lead * per_quarter)
     place = jnp.arange(groups, dtype=jnp.int32) ^ turn
     last_rows = jnp.arange(per_quarter, dtype=jnp.int32) + per_quarter
-    inverse = lax.rsqrt(squares[last_rows ^ turn].reshape(quarter) / D + 1e-05)[:, None]
-
-    n_units = gate_weight.shape[1] // UNIT
-    edges = [n_units * i // CHUNKS for i in range(CHUNKS + 1)]
+    unit = gate_weight.shape[1] // sum(CHUNK_UNITS)
+    edges = [sum(CHUNK_UNITS[:i]) for i in range(len(CHUNK_UNITS) + 1)]
     f32 = jnp.float32
-    total = None
-    for start, stop in zip(edges[:-1], edges[1:]):
-        first, second, send = gate_up(place, blocks, gate_weight, up_weight, start, stop - start)
+    passed, chunks = [], []
+    inverse = None
+    for k, units in enumerate(CHUNK_UNITS):
+        after = [passed[k - 2 - i][i] for i in range(min(k - 1, chips - 1))]
+        ride = squares[None, :] if k == 0 else None
+        first, second, send, *rides = gate_up(
+            place, blocks, gate_weight, up_weight, unit, edges[k], units, after, ride
+        )
+        if k == 0:
+            squares = rides[0][0]
+            squares = [squares] + [partner(squares, "grp", i) for i in range(1, groups)]
+            squares = jnp.stack(squares)[last_rows ^ turn].reshape(quarter, 1)
+            inverse = lax.rsqrt(squares / D + 1e-05)
         other = partner(send, "blk", 1)
-        first = first + other[:, :quarter].astype(f32)
-        second = second + other[:, quarter:].astype(f32)
+        with_other = [first + other[:, :quarter].astype(f32), second + other[:, quarter:].astype(f32)]
         flow = None
+        passed.append([])
         for step in range(1, chips):
-            own = first if step <= chips // 2 else second
-            flow = own if flow is None else own + flow.astype(f32)
-            flow = along_line(flow.astype(jnp.bfloat16), step)
-        sums = second + flow.astype(f32)
-        gate, up_part = sums[0] * inverse, sums[1] * inverse
-        hidden = (jax.nn.silu(gate) * up_part).astype(jnp.bfloat16)
+            own = with_other[step > chips // 2]
+            flow = (own if flow is None else own + flow.astype(f32)).astype(jnp.bfloat16)
+            passed[k].append(flow)
+            flow = along_line(flow, step)
+        hidden = hidden_units(flow, second, other, inverse)
         halves = [hidden, None]
         for step in range(1, chips):
+            passed[k].append(hidden)
             hidden = along_line(hidden, step)
             half = step // (chips // 2)
             here = (chip == step) | (chip == chips - 1 - step)
             halves[half] = hidden if halves[half] is None else jnp.where(here, hidden, halves[half])
         halves = [halves[1], halves[0]]
-        theirs = [partner(half, "blk", 1) for half in halves]
-        total = down(halves + theirs, down_weight, total, start, stop - start)
+        chunks.append(halves + [partner(half, "blk", 1) for half in halves])
+    total = None
+    for k, units in enumerate(CHUNK_UNITS):
+        after = [passed[k + 1 + i][-i] for i in range(1, chips - 1) if k + 1 + i < len(passed)]
+        total = down(chunks[k], down_weight, total, unit, edges[k], units, after)
 
     terms = total.reshape(groups, rows, -1)
     own = lax.dynamic_index_in_dim(terms, turn, 0, keepdims=False)

time: 237 us -> 235 us (level)
  waiting for transfers between devices: 103 us -> 68.1 us
  other arithmetic: 7.58 us -> 18.3 us
  Pallas kernels: 63.7 us -> 73.5 us
  starting transfers between devices: 53.9 us -> 61.5 us
  local copies, waits for them, and re-layouts: 3.75 us -> 9.36 us
    ppermute x24, waiting for transfers between devices: 82.9 us -> 47.7 us  [along_line(): lax.ppermute(x, 'blk', [(2 * a + c, 2 * b + c) for a, b in hops for c in...]
    pallas_call x4 -> x8, Pallas kernels: 35.3 us -> 51.9 us  [the longest x4 32.9 us: gate_up(): pl.pallas_call(functools.partial(gate_up_kernel, len(blocks), len(blocks)...]
    ppermute x24, starting transfers between devices: 32.5 us -> 43.2 us  [along_line(): lax.ppermute(x, 'blk', [(2 * a + c, 2 * b + c) for a, b in hops for c in...]
    convert_element_type x14 -> x12, other arithmetic: 2.08 us -> 11.1 us  [on_device(): (own if flow is None else own + flow.astype(f32)).astype(jnp.bfloat16)]
    pallas_call x4, Pallas kernels: 28.4 us -> 21.6 us  [down(): pl.pallas_call(functools.partial(down_kernel, has_total), grid=(units,),...]
    unnamed x16 -> x70, local copies, waits for them, and re-layouts: 2.13 us -> 7.13 us
    ppermute x24, starting transfers between devices: 21.4 us -> 18.3 us  [partner(): lax.ppermute(x, axis, [(i, i ^ distance) for i in range(lax.axis_size(axi...]
  transfers between devices with their start and end apart: 48 -> 48, of which waited for: 23 -> 17; matrix products, arithmetic and copies ran while one was open for 1% -> 6% of each run, Pallas kernels for 20% -> 26%
where the time goes in v2:
time: 235 us; the launch traced here: 233 us
  Pallas kernels  73.5 us (31%)
  waiting for transfers between devices  68.1 us (29%)
  starting transfers between devices  61.5 us (26%)
  other arithmetic  18.3 us (8%)
  local copies, waits for them, and re-layouts  9.36 us (4%)
    ppermute x24, waiting for transfers between devices, along_line(): lax.ppermute(x, 'blk', [(2 * a + c, 2 * b + c) for a, b in hops for c in...  47.7 us
    ppermute x24, starting transfers between devices, along_line(): lax.ppermute(x, 'blk', [(2 * a + c, 2 * b + c) for a, b in hops for c in...  43.2 us
    pallas_call x4, Pallas kernels, gate_up(): pl.pallas_call(functools.partial(gate_up_kernel, len(blocks), len(blocks)...  32.9 us
    pallas_call x4, Pallas kernels, down(): pl.pallas_call(functools.partial(down_kernel, has_total), grid=(units,),...  21.6 us
    ppermute x24, waiting for transfers between devices, partner(): lax.ppermute(x, axis, [(i, i ^ distance) for i in range(lax.axis_size(axi...  20.4 us
    pallas_call x4, Pallas kernels, hidden_units(): pl.pallas_call(hidden_kernel, grid=(cols // tile,), in_specs=[pl.BlockSpe...  19 us
    ppermute x24, starting transfers between devices, partner(): lax.ppermute(x, axis, [(i, i ^ distance) for i in range(lax.axis_size(axi...  18.3 us
    convert_element_type x12, other arithmetic, on_device(): (own if flow is None else own + flow.astype(f32)).astype(jnp.bfloat16)  11.1 us
  transfers between devices with their start and end apart: 48, of which 17 were waited for; matrix products, arithmetic and copies ran while one was open for 6% of the time, Pallas kernels for 26%

profile of v2, /device:TPU:0, one launch (start us, length us, event | category | flops | bytes accessed | tf_op | source)
XLA Modules:
  0.0 233.4 jit_solution(15526263701126409368)
XLA Ops:
  2.4 1.3 dynamic-slice_convert_fusion.3
  6.7 3.9 %collective-permute-start.2 = (bf16[64,2048]{1,0:T(8,128)(2,1)S(1)}, bf16[64,2048]{1,0:T(8,128)(2,1)S(1)}, u32[]{:S(2)}, u32[]{:S(2)}) collective-permute-start(bf16[64,2048]{1,0:T(8,128)(2,1)S(1)} %get-tuple-element.48.refs_0_), channel_id=1, source_target_pairs={{0,24},{8,16},{16,8},{24,0},{1,25},{9,17},{17,9},{25,1},{2,26},{10... | collective-permute-start | bytes 786440 | tf_op jit(solution)/shard_map/ppermute | solution.py:19
  11.2 1.1 collective-permute-done.4
  12.3 2.1 collective-permute-start.5
  14.4 1.5 collective-permute-done.5
  15.9 3.0 %collective-permute-start.6 = (f32[64]{0:T(128)S(1)}, f32[64]{0:T(128)S(1)}, u32[]{:S(2)}, u32[]{:S(2)}) collective-permute-start(f32[64]{0:T(128)S(1)} %add.139), channel_id=1, source_target_pairs={{0,4},{1,5},{2,6},{3,7},{4,0},{5,1},{6,2},{7,3},{8,12},{9,13},{10,... | collective-permute-start | bytes 776 | tf_op jit(solution)/shard_map/ppermute | solution.py:19
  18.9 1.5 collective-permute-done.6
  20.4 2.1 collective-permute-done.1.refs_2_
  22.8 8.1 %shard_map.110 = (f32[2,64,1536]{2,1,0:T(8,128)S(1)}, f32[2,64,1536]{2,1,0:T(8,128)S(1)}, bf16[2,128,1536]{2,1,0:T(8,128)(2,1)}, f32[1,64]{1,0:T(1,128)S(1)}) custom-call(s32[4]{0:T(128)S(1)} %iota_xor_fusion.place_ref, bf16[64,2048]{1,0:T(8,128)(2,1)S(1)} %get-tuple-element.48.refs_0_, bf16[64,2048]{1,0:T(8,128)(2,1)S(1)} %collective-permute-done.refs_1_, ...), custom_call_target="tpu_custom_call" | custom-call | flops 3221225472 | bytes 18350080 | tf_op jit(solution)/shard_map/pallas_call | solution.py:56
  32.6 1.5 collective-permute-start.15
  34.1 1.5 collective-permute-start.14
  36.1 9.6 %shard_map.109 = (f32[2,64,2048]{2,1,0:T(8,128)S(1)}, f32[2,64,2048]{2,1,0:T(8,128)S(1)}, bf16[2,128,2048]{2,1,0:T(8,128)(2,1)}) custom-call(s32[4]{0:T(128)S(1)} %iota_xor_fusion.place_ref, bf16[64,2048]{1,0:T(8,128)(2,1)S(1)} %get-tuple-element.48.refs_0_, bf16[64,2048]{1,0:T(8,128)(2,1)S(1)} %collective-permute-done.refs_1_, ...), custom_call_target="tpu_custom_call" | custom-call | flops 4294967296 | bytes 24117248 | tf_op jit(solution)/shard_map/pallas_call | solution.py:56
  45.7 1.0 copy-done.3
  46.7 1.0 copy-done.5
  47.8 4.2 %collective-permute-start.8 = (bf16[2,64,1536]{2,1,0:T(8,128)(2,1)S(1)}, bf16[2,64,1536]{2,1,0:T(8,128)(2,1)}, u32[]{:S(2)}, u32[]{:S(2)}) collective-permute-start(bf16[2,64,1536]{2,1,0:T(8,128)(2,1)S(1)} %fusion.4.refs_6_), channel_id=1, source_target_pairs={{0,2},{1,3},{6,4},{7,5},{8,10},{9,11},{14,12},{15,13},{16,18},{17,... | collective-permute-start | bytes 1179656 | tf_op jit(solution)/shard_map/ppermute | solution.py:25
  52.8 7.3 %shard_map.113 = (f32[2,64,1536]{2,1,0:T(8,128)S(1)}, f32[2,64,1536]{2,1,0:T(8,128)S(1)}, bf16[2,128,1536]{2,1,0:T(8,128)(2,1)S(1)}) custom-call(s32[4]{0:T(128)S(1)} %iota_xor_fusion.place_ref, bf16[64,2048]{1,0:T(8,128)(2,1)S(1)} %get-tuple-element.48.refs_0_, bf16[64,2048]{1,0:T(8,128)(2,1)S(1)} %collective-permute-done.refs_1_, ...), custom_call_target="tpu_custom_call" | custom-call | flops 3221225472 | bytes 18350080 | tf_op jit(solution)/shard_map/pallas_call | solution.py:56
  60.4 1.8 add_convert_fusion.7.refs_7_
  62.9 1.2 fusion.3.refs_6_
  64.1 6.8 %collective-permute-start.30 = (bf16[2,64,2048]{2,1,0:T(8,128)(2,1)S(1)}, bf16[2,64,2048]{2,1,0:T(8,128)(2,1)S(1)}, u32[]{:S(2)}, u32[]{:S(2)}) collective-permute-start(bf16[2,64,2048]{2,1,0:T(8,128)(2,1)S(1)} %fusion.3.refs_6_), channel_id=1, source_target_pairs={{0,2},{1,3},{6,4},{7,5},{8,10},{9,11},{14,12},{15,13},{16,18},{17,... | collective-permute-start | bytes 1572872 | tf_op jit(solution)/shard_map/ppermute | solution.py:25
  70.9 8.0 %shard_map.111 = (f32[2,64,1536]{2,1,0:T(8,128)S(1)}, f32[2,64,1536]{2,1,0:T(8,128)S(1)}, bf16[2,128,1536]{2,1,0:T(8,128)(2,1)}) custom-call(s32[4]{0:T(128)S(1)} %iota_xor_fusion.place_ref, bf16[64,2048]{1,0:T(8,128)(2,1)S(1)} %get-tuple-element.48.refs_0_, bf16[64,2048]{1,0:T(8,128)(2,1)S(1)} %collective-permute-done.refs_1_, ...), custom_call_target="tpu_custom_call" | custom-call | flops 3221225472 | bytes 18350080 | tf_op jit(solution)/shard_map/pallas_call | solution.py:56
  79.1 1.3 collective-permute-start.39
  80.5 5.3 %collective-permute-start.22 = (bf16[2,64,1536]{2,1,0:T(8,128)(2,1)S(1)}, bf16[2,64,1536]{2,1,0:T(8,128)(2,1)S(1)}, u32[]{:S(2)}, u32[]{:S(2)}) collective-permute-start(bf16[2,64,1536]{2,1,0:T(8,128)(2,1)S(1)} %fusion.6), channel_id=1, source_target_pairs={{0,2},{1,3},{6,4},{7,5},{8,10},{9,11},{14,12},{15,13},{16,18},{17,... | collective-permute-start | bytes 1179656 | tf_op jit(solution)/shard_map/ppermute | solution.py:25
  85.8 2.0 add_convert_fusion.1
  87.9 1.5 collective-permute-start.31
  89.3 3.3 %collective-permute-done.39.flow_ref = bf16[2,64,1536]{2,1,0:T(8,128)(2,1)} collective-permute-done((bf16[2,64,1536]{2,1,0:T(8,128)(2,1)S(1)}, bf16[2,64,1536]{2,1,0:T(8,128)(2,1)}, u32[]{:S(2)}, u32[]{:S(2)}) %collective-permute-start.39) | collective-permute-done | bytes 393248 | tf_op jit(solution)/shard_map/ppermute | solution.py:25
  92.6 4.4 %shard_map.116 = bf16[64,1536]{1,0:T(8,128)(2,1)} custom-call(bf16[2,64,1536]{2,1,0:T(8,128)(2,1)} %collective-permute-done.39.flow_ref, f32[2,64,1536]{2,1,0:T(8,128)} %copy-done.11, bf16[2,128,1536]{2,1,0:T(8,128)(2,1)} %copy-done.21, f32[64,1]{1,0:T(8,128)} %copy.15.inverse_ref), custom_call_target="tpu_custom_call" | custom-call | flops 1572864 | bytes 1769472 | tf_op jit(solution)/shard_map/pallas_call | solution.py:98
  97.0 1.5 collective-permute-start.40
  99.4 1.2 fusion.5
  100.6 3.0 %collective-permute-start.10 = (bf16[2,64,1536]{2,1,0:T(8,128)(2,1)S(1)}, bf16[2,64,1536]{2,1,0:T(8,128)(2,1)S(1)}, u32[]{:S(2)}, u32[]{:S(2)}) collective-permute-start(bf16[2,64,1536]{2,1,0:T(8,128)(2,1)S(1)} %fusion.5), channel_id=1, source_target_pairs={{0,2},{1,3},{6,4},{7,5},{8,10},{9,11},{14,12},{15,13},{16,18},{17,... | collective-permute-start | bytes 1179656 | tf_op jit(solution)/shard_map/ppermute | solution.py:25
  103.6 1.4 add_convert_fusion
  105.0 1.3 collective-permute-start.32
  108.0 1.3 collective-permute-start.24
  109.3 1.3 collective-permute-start.42
  111.5 1.1 add_convert_fusion.6
  113.3 19.2 %collective-permute-done.42 = bf16[64,1536]{1,0:T(8,128)(2,1)S(1)} collective-permute-done((bf16[64,1536]{1,0:T(8,128)(2,1)S(1)}, bf16[64,1536]{1,0:T(8,128)(2,1)S(1)}, u32[]{:S(2)}, u32[]{:S(2)}) %collective-permute-start.42) | collective-permute-done | bytes 196640 | tf_op jit(solution)/shard_map/ppermute | solution.py:25
  132.6 5.6 %shard_map.115 = bf16[64,2048]{1,0:T(8,128)(2,1)} custom-call(bf16[2,64,2048]{2,1,0:T(8,128)(2,1)} %collective-permute-done.32.flow_ref, f32[2,64,2048]{2,1,0:T(8,128)} %copy-done.5, bf16[2,128,2048]{2,1,0:T(8,128)(2,1)} %collective-permute-done.3.other_ref, f32[64,1]{1,0:T(8,128)} %copy.15.inverse_ref), custom_call_target="tpu_custom_call" | custom-call | flops 2097152 | bytes 2359296 | tf_op jit(solution)/shard_map/pallas_call | solution.py:98
  138.2 2.3 collective-permute-start.33
  141.2 4.4 %shard_map.114 = bf16[64,1536]{1,0:T(8,128)(2,1)} custom-call(bf16[2,64,1536]{2,1,0:T(8,128)(2,1)} %copy-done.30, f32[2,64,1536]{2,1,0:T(8,128)} %copy-done.9, bf16[2,128,1536]{2,1,0:T(8,128)(2,1)} %copy-done.20, f32[64,1]{1,0:T(8,128)} %copy.15.inverse_ref), custom_call_target="tpu_custom_call" | custom-call | flops 1572864 | bytes 1769472 | tf_op jit(solution)/shard_map/pallas_call | solution.py:98
  145.7 2.0 collective-permute-start.25
  147.7 1.2 add_convert_fusion.5
  148.8 1.3 collective-permute-start.12
  150.9 1.2 collective-permute-done.25
  152.8 9.2 %collective-permute-done.12.flow_ref = bf16[2,64,1536]{2,1,0:T(8,128)(2,1)S(1)} collective-permute-done((bf16[2,64,1536]{2,1,0:T(8,128)(2,1)S(1)}, bf16[2,64,1536]{2,1,0:T(8,128)(2,1)S(1)}, u32[]{:S(2)}, u32[]{:S(2)}) %collective-permute-start.12) | collective-permute-done | bytes 393248 | tf_op jit(solution)/shard_map/ppermute | solution.py:25
  162.8 4.5 %shard_map.112 = bf16[64,1536]{1,0:T(8,128)(2,1)} custom-call(bf16[2,64,1536]{2,1,0:T(8,128)(2,1)} %copy-done.31, f32[2,64,1536]{2,1,0:T(8,128)} %copy-done.7, bf16[2,128,1536]{2,1,0:T(8,128)(2,1)} %collective-permute-done.9.other_ref, f32[64,1]{1,0:T(8,128)} %copy.15.inverse_ref), custom_call_target="tpu_custom_call" | custom-call | flops 1572864 | bytes 1769472 | tf_op jit(solution)/shard_map/pallas_call | solution.py:98
  167.2 1.4 collective-permute-start.16
  168.8 1.3 collective-permute-start.27
  170.1 2.7 %collective-permute-done.16.refs_6_ = bf16[64,1536]{1,0:T(8,128)(2,1)S(1)} collective-permute-done((bf16[64,1536]{1,0:T(8,128)(2,1)}, bf16[64,1536]{1,0:T(8,128)(2,1)S(1)}, u32[]{:S(2)}, u32[]{:S(2)}) %collective-permute-start.16) | collective-permute-done | bytes 196640 | tf_op jit(solution)/shard_map/ppermute | solution.py:25
  172.9 1.3 collective-permute-start.35
  174.1 1.0 broadcast_select_fusion.4.refs_1_
  175.1 3.3 %collective-permute-done.27 = bf16[64,1536]{1,0:T(8,128)(2,1)S(1)} collective-permute-done((bf16[64,1536]{1,0:T(8,128)(2,1)S(1)}, bf16[64,1536]{1,0:T(8,128)(2,1)S(1)}, u32[]{:S(2)}, u32[]{:S(2)}) %collective-permute-start.27) | collective-permute-done | bytes 196640 | tf_op jit(solution)/shard_map/ppermute | solution.py:25
  179.9 5.0 %shard_map.117.refs_5_ = f32[256,2048]{1,0:T(8,128)S(1)} custom-call(bf16[64,1536]{1,0:T(8,128)(2,1)S(1)} %broadcast_select_fusion.5.refs_0_, bf16[64,1536]{1,0:T(8,128)(2,1)S(1)} %broadcast_select_fusion.2.refs_1_, bf16[64,1536]{1,0:T(8,128)(2,1)S(1)} %collective-permute-done.43.refs_2_, bf16[64,1536]{1,0:T(8,128)(2,1)S(1)} %collective-permute-done.44.refs_3_, ...), custom_call_target="tpu_custom_call" | custom-call | flops 1610612736 | bytes 10485760 | tf_op jit(solution)/shard_map/pallas_call | solution.py:137
  185.0 1.3 collective-permute-start.18
  186.4 7.8 %collective-permute-done.18 = bf16[64,1536]{1,0:T(8,128)(2,1)S(1)} collective-permute-done((bf16[64,1536]{1,0:T(8,128)(2,1)S(1)}, bf16[64,1536]{1,0:T(8,128)(2,1)S(1)}, u32[]{:S(2)}, u32[]{:S(2)}) %collective-permute-start.18) | collective-permute-done | bytes 196640 | tf_op jit(solution)/shard_map/ppermute | solution.py:25
  194.8 0.9 collective-permute-done.36.refs_2_
  195.7 6.3 %shard_map.118.refs_5_ = f32[256,2048]{1,0:T(8,128)S(1)} custom-call(bf16[64,2048]{1,0:T(8,128)(2,1)S(1)} %broadcast_select_fusion.1.refs_0_, bf16[64,2048]{1,0:T(8,128)(2,1)S(1)} %broadcast_select_fusion.refs_1_, bf16[64,2048]{1,0:T(8,128)(2,1)S(1)} %collective-permute-done.36.refs_2_, ...), custom_call_target="tpu_custom_call", output_to_operand_aliasing={{}: (5, {})} | custom-call | flops 2147483648 | bytes 12582912 | tf_op jit(solution)/shard_map/pallas_call | solution.py:137
  202.0 5.2 %shard_map.119.refs_5_ = f32[256,2048]{1,0:T(8,128)S(1)} custom-call(bf16[64,1536]{1,0:T(8,128)(2,1)S(1)} %broadcast_select_fusion.6.refs_0_, bf16[64,1536]{1,0:T(8,128)(2,1)S(1)} %broadcast_select_fusion.3.refs_1_, bf16[64,1536]{1,0:T(8,128)(2,1)S(1)} %collective-permute-done.28.refs_2_, ...), custom_call_target="tpu_custom_call", output_to_operand_aliasing={{}: (5, {})} | custom-call | flops 1610612736 | bytes 10485760 | tf_op jit(solution)/shard_map/pallas_call | solution.py:137
  207.2 5.2 %shard_map.120 = f32[256,2048]{1,0:T(8,128)S(1)} custom-call(bf16[64,1536]{1,0:T(8,128)(2,1)S(1)} %broadcast_select_fusion.7.refs_0_, bf16[64,1536]{1,0:T(8,128)(2,1)S(1)} %broadcast_select_fusion.4.refs_1_, bf16[64,1536]{1,0:T(8,128)(2,1)S(1)} %collective-permute-done.19.refs_2_, ...), custom_call_target="tpu_custom_call", output_to_operand_aliasing={{}: (5, {})} | custom-call | flops 1610612736 | bytes 10485760 | tf_op jit(solution)/shard_map/pallas_call | solution.py:137
  212.5 1.3 copy-done.2
  214.6 1.5 collective-permute-start.45
  216.1 1.4 collective-permute-start.47
  218.1 6.0 %collective-permute-done.45 = bf16[64,2048]{1,0:T(8,128)(2,1)} collective-permute-done((bf16[64,2048]{1,0:T(8,128)(2,1)}, bf16[64,2048]{1,0:T(8,128)(2,1)}, u32[]{:S(2)}, u32[]{:S(2)}) %collective-permute-start.45) | collective-permute-done | bytes 262176 | tf_op jit(solution)/shard_map/ppermute | solution.py:19
  224.1 5.8 %collective-permute-done.47 = bf16[64,2048]{1,0:T(8,128)(2,1)} collective-permute-done((bf16[64,2048]{1,0:T(8,128)(2,1)S(1)}, bf16[64,2048]{1,0:T(8,128)(2,1)}, u32[]{:S(2)}, u32[]{:S(2)}) %collective-permute-start.47) | collective-permute-done | bytes 262176 | tf_op jit(solution)/shard_map/ppermute | solution.py:19
  229.8 1.2 collective-permute-done.46
  231.0 2.4 %fusion.9 = f32[64,2048]{1,0:T(8,128)} fusion(bf16[64,2048]{1,0:T(8,128)(2,1)} %collective-permute-done.47, bf16[64,2048]{1,0:T(8,128)(2,1)} %collective-permute-done.46, bf16[64,2048]{1,0:T(8,128)(2,1)} %collective-permute-done.45, f32[4,64,2048]{2,1,0:T(8,128)} %bitcast.52, s32[]{:T(128)S(6)} %select_n.119, f32[8,8,16,128]{3,2,1,0:T(8,128)S(1)} %bitcast.57, ...), kind=kLoop, calls=%fused_computation.25 | loop fusion | flops 1179648 | bytes 2621444 | tf_op jit(solution)/shard_map/add | solution.py:292
  (154 shorter events, 21.3 us)
Async XLA Ops:
  6.7 13.7 %collective-permute-start.2 = (bf16[64,2048]{1,0:T(8,128)(2,1)S(1)}, bf16[64,2048]{1,0:T(8,128)(2,1)S(1)}, u32[]{:S(2)}, u32[]{:S(2)}) collective-permute-start(bf16[64,2048]{1,0:T(8,128)(2,1)S(1)} %get-tuple-element.48.refs_0_), channel_id=1, source_target_pairs={{0,24},{8,16},{16,8},{24,0},{1,25},{9,17},{17,9},{25,1},{2,26},{10... | collective-permute-start | bytes 786440 | tf_op jit(solution)/shard_map/ppermute | solution.py:19
  10.6 11.9 %collective-permute-start.1 = (bf16[64,2048]{1,0:T(8,128)(2,1)S(1)}, bf16[64,2048]{1,0:T(8,128)(2,1)S(1)}, u32[]{:S(2)}, u32[]{:S(2)}) collective-permute-start(bf16[64,2048]{1,0:T(8,128)(2,1)S(1)} %get-tuple-element.48.refs_0_), channel_id=1, source_target_pairs={{0,16},{8,24},{16,0},{24,8},{1,17},{9,25},{17,1},{25,9},{2,18},{10... | collective-permute-start | bytes 786440 | tf_op jit(solution)/shard_map/ppermute | solution.py:19
  11.1 11.7 %collective-permute-start = (bf16[64,2048]{1,0:T(8,128)(2,1)S(1)}, bf16[64,2048]{1,0:T(8,128)(2,1)S(1)}, u32[]{:S(2)}, u32[]{:S(2)}) collective-permute-start(bf16[64,2048]{1,0:T(8,128)(2,1)S(1)} %get-tuple-element.48.refs_0_), channel_id=1, source_target_pairs={{0,8},{8,0},{16,24},{24,16},{1,9},{9,1},{17,25},{25,17},{2,10},{10... | collective-permute-start | bytes 786440 | tf_op jit(solution)/shard_map/ppermute | solution.py:19
  11.2 1.1 collective-permute-start.4
  12.3 3.6 %collective-permute-start.5 = (f32[64]{0:T(128)S(1)}, f32[64]{0:T(128)S(1)}, u32[]{:S(2)}, u32[]{:S(2)}) collective-permute-start(f32[64]{0:T(128)S(1)} %add.138), channel_id=1, source_target_pairs={{0,2},{1,3},{2,0},{3,1},{4,6},{5,7},{6,4},{7,5},{8,10},{9,11},{10,... | collective-permute-start | bytes 776 | tf_op jit(solution)/shard_map/ppermute | solution.py:19
  15.9 4.6 %collective-permute-start.6 = (f32[64]{0:T(128)S(1)}, f32[64]{0:T(128)S(1)}, u32[]{:S(2)}, u32[]{:S(2)}) collective-permute-start(f32[64]{0:T(128)S(1)} %add.139), channel_id=1, source_target_pairs={{0,4},{1,5},{2,6},{3,7},{4,0},{5,1},{6,2},{7,3},{8,12},{9,13},{10,... | collective-permute-start | bytes 776 | tf_op jit(solution)/shard_map/ppermute | solution.py:19
  32.6 15.0 %collective-permute-start.7 = (bf16[2,128,1536]{2,1,0:T(8,128)(2,1)}, bf16[2,128,1536]{2,1,0:T(8,128)(2,1)S(1)}, u32[]{:S(2)}, u32[]{:S(2)}) collective-permute-start(bf16[2,128,1536]{2,1,0:T(8,128)(2,1)} %get-tuple-element.21), channel_id=1, source_target_pairs={{0,1},{1,0},{2,3},{3,2},{4,5},{5,4},{6,7},{7,6},{8,9},{9,8},{10,11... | collective-permute-start | bytes 2359304 | tf_op jit(solution)/shard_map/ppermute | solution.py:19
  32.6 15.1 %copy-start.16 = (f32[2,64,1536]{2,1,0:T(8,128)S(1)}, f32[2,64,1536]{2,1,0:T(8,128)}, u32[]{:S(2)}) copy-start(f32[2,64,1536]{2,1,0:T(8,128)} %copy-done.15) | copy-start | bytes 2359300
  32.6 15.0 %collective-permute-start.15 = (f32[64]{0:T(128)S(1)}, f32[64]{0:T(128)S(1)}, u32[]{:S(2)}, u32[]{:S(2)}) collective-permute-start(f32[64]{0:T(128)S(1)} %bitcast.53), channel_id=1, source_target_pairs={{0,24},{8,16},{16,8},{24,0},{1,25},{9,17},{17,9},{25,1},{2,26},{10... | collective-permute-start | bytes 776 | tf_op jit(solution)/shard_map/ppermute | solution.py:19
  34.1 13.6 %collective-permute-start.14 = (f32[64]{0:T(128)S(1)}, f32[64]{0:T(128)S(1)}, u32[]{:S(2)}, u32[]{:S(2)}) collective-permute-start(f32[64]{0:T(128)S(1)} %bitcast.54), channel_id=1, source_target_pairs={{0,16},{8,24},{16,0},{24,8},{1,17},{9,25},{17,1},{25,9},{2,18},{10... | collective-permute-start | bytes 776 | tf_op jit(solution)/shard_map/ppermute | solution.py:19
  35.6 12.1 %collective-permute-start.13 = (f32[64]{0:T(128)S(1)}, f32[64]{0:T(128)S(1)}, u32[]{:S(2)}, u32[]{:S(2)}) collective-permute-start(f32[64]{0:T(128)S(1)} %bitcast.55), channel_id=1, source_target_pairs={{0,8},{8,0},{16,24},{24,16},{1,9},{9,1},{17,25},{25,17},{2,10},{10... | collective-permute-start | bytes 776 | tf_op jit(solution)/shard_map/ppermute | solution.py:19
  47.6 15.2 %collective-permute-start.3 = (bf16[2,128,2048]{2,1,0:T(8,128)(2,1)}, bf16[2,128,2048]{2,1,0:T(8,128)(2,1)}, u32[]{:S(2)}, u32[]{:S(2)}) collective-permute-start(bf16[2,128,2048]{2,1,0:T(8,128)(2,1)} %get-tuple-element.19), channel_id=1, source_target_pairs={{0,1},{1,0},{2,3},{3,2},{4,5},{5,4},{6,7},{7,6},{8,9},{9,8},{10,11... | collective-permute-start | bytes 3145736 | tf_op jit(solution)/shard_map/ppermute | solution.py:19
  47.7 12.3 %copy-start.21 = (bf16[2,128,1536]{2,1,0:T(8,128)(2,1)}, bf16[2,128,1536]{2,1,0:T(8,128)(2,1)S(1)}, u32[]{:S(2)}) copy-start(bf16[2,128,1536]{2,1,0:T(8,128)(2,1)S(1)} %collective-permute-done.7.other_ref) | copy-start | bytes 2359300
  47.8 12.6 %collective-permute-start.8 = (bf16[2,64,1536]{2,1,0:T(8,128)(2,1)S(1)}, bf16[2,64,1536]{2,1,0:T(8,128)(2,1)}, u32[]{:S(2)}, u32[]{:S(2)}) collective-permute-start(bf16[2,64,1536]{2,1,0:T(8,128)(2,1)S(1)} %fusion.4.refs_6_), channel_id=1, source_target_pairs={{0,2},{1,3},{6,4},{7,5},{8,10},{9,11},{14,12},{15,13},{16,18},{17,... | collective-permute-start | bytes 1179656 | tf_op jit(solution)/shard_map/ppermute | solution.py:25
  60.1 20.4 %copy-start.18 = (f32[2,64,1536]{2,1,0:T(8,128)}, f32[2,64,1536]{2,1,0:T(8,128)S(1)}, u32[]{:S(2)}) copy-start(f32[2,64,1536]{2,1,0:T(8,128)S(1)} %get-tuple-element.28) | copy-start | bytes 2359300
  60.1 20.3 %collective-permute-start.21 = (bf16[2,128,1536]{2,1,0:T(8,128)(2,1)S(1)}, bf16[2,128,1536]{2,1,0:T(8,128)(2,1)S(1)}, u32[]{:S(2)}, u32[]{:S(2)}) collective-permute-start(bf16[2,128,1536]{2,1,0:T(8,128)(2,1)S(1)} %get-tuple-element.27), channel_id=1, source_target_pairs={{0,1},{1,0},{2,3},{3,2},{4,5},{5,4},{6,7},{7,6},{8,9},{9,8},{10,11... | collective-permute-start | bytes 2359304 | tf_op jit(solution)/shard_map/ppermute | solution.py:19
  62.2 16.7 %collective-permute-start.38 = (bf16[2,64,1536]{2,1,0:T(8,128)(2,1)S(1)}, bf16[2,64,1536]{2,1,0:T(8,128)(2,1)S(1)}, u32[]{:S(2)}, u32[]{:S(2)}) collective-permute-start(bf16[2,64,1536]{2,1,0:T(8,128)(2,1)S(1)} %add_convert_fusion.7.refs_7_), channel_id=1, source_target_pairs={{2,4},{3,5},{4,2},{5,3},{10,12},{11,13},{12,10},{13,11},{18,20},{1... | collective-permute-start | bytes 1179656 | tf_op jit(solution)/shard_map/ppermute | solution.py:25
  64.1 14.9 %copy-start.12 = (f32[2,64,1536]{2,1,0:T(8,128)S(1)}, f32[2,64,1536]{2,1,0:T(8,128)}, u32[]{:S(2)}) copy-start(f32[2,64,1536]{2,1,0:T(8,128)} %copy-done.11) | copy-start | bytes 2359300
  64.1 14.9 %copy-start.22 = (bf16[2,128,1536]{2,1,0:T(8,128)(2,1)S(1)}, bf16[2,128,1536]{2,1,0:T(8,128)(2,1)}, u32[]{:S(2)}) copy-start(bf16[2,128,1536]{2,1,0:T(8,128)(2,1)} %copy-done.21) | copy-start | bytes 2359300
  64.1 21.7 %collective-permute-start.30 = (bf16[2,64,2048]{2,1,0:T(8,128)(2,1)S(1)}, bf16[2,64,2048]{2,1,0:T(8,128)(2,1)S(1)}, u32[]{:S(2)}, u32[]{:S(2)}) collective-permute-start(bf16[2,64,2048]{2,1,0:T(8,128)(2,1)S(1)} %fusion.3.refs_6_), channel_id=1, source_target_pairs={{0,2},{1,3},{6,4},{7,5},{8,10},{9,11},{14,12},{15,13},{16,18},{17,... | collective-permute-start | bytes 1572872 | tf_op jit(solution)/shard_map/ppermute | solution.py:25
  78.9 8.9 %copy-start.7 = (f32[2,64,1536]{2,1,0:T(8,128)}, f32[2,64,1536]{2,1,0:T(8,128)S(1)}, u32[]{:S(2)}) copy-start(f32[2,64,1536]{2,1,0:T(8,128)S(1)} %get-tuple-element.22.own_ref) | copy-start | bytes 2359300
  78.9 8.9 %copy-start.13 = (f32[2,64,1536]{2,1,0:T(8,128)}, f32[2,64,1536]{2,1,0:T(8,128)S(1)}, u32[]{:S(2)}) copy-start(f32[2,64,1536]{2,1,0:T(8,128)S(1)} %get-tuple-element.24) | copy-start | bytes 2359300
  78.9 20.5 %collective-permute-start.9 = (bf16[2,128,1536]{2,1,0:T(8,128)(2,1)}, bf16[2,128,1536]{2,1,0:T(8,128)(2,1)}, u32[]{:S(2)}, u32[]{:S(2)}) collective-permute-start(bf16[2,128,1536]{2,1,0:T(8,128)(2,1)} %get-tuple-element.23), channel_id=1, source_target_pairs={{0,1},{1,0},{2,3},{3,2},{4,5},{5,4},{6,7},{7,6},{8,9},{9,8},{10,11... | collective-permute-start | bytes 2359304 | tf_op jit(solution)/shard_map/ppermute | solution.py:19
  79.1 13.5 %collective-permute-start.39 = (bf16[2,64,1536]{2,1,0:T(8,128)(2,1)S(1)}, bf16[2,64,1536]{2,1,0:T(8,128)(2,1)}, u32[]{:S(2)}, u32[]{:S(2)}) collective-permute-start(bf16[2,64,1536]{2,1,0:T(8,128)(2,1)S(1)} %add_convert_fusion.2), channel_id=1, source_target_pairs={{4,6},{5,7},{2,0},{3,1},{12,14},{13,15},{10,8},{11,9},{20,22},{21,... | collective-permute-start | bytes 1179656 | tf_op jit(solution)/shard_map/ppermute | solution.py:25
  80.4 26.7 %copy-start.20 = (bf16[2,128,1536]{2,1,0:T(8,128)(2,1)}, bf16[2,128,1536]{2,1,0:T(8,128)(2,1)S(1)}, u32[]{:S(2)}) copy-start(bf16[2,128,1536]{2,1,0:T(8,128)(2,1)S(1)} %collective-permute-done.21.other_ref) | copy-start | bytes 2359300
  80.5 18.0 %collective-permute-start.22 = (bf16[2,64,1536]{2,1,0:T(8,128)(2,1)S(1)}, bf16[2,64,1536]{2,1,0:T(8,128)(2,1)S(1)}, u32[]{:S(2)}, u32[]{:S(2)}) collective-permute-start(bf16[2,64,1536]{2,1,0:T(8,128)(2,1)S(1)} %fusion.6), channel_id=1, source_target_pairs={{0,2},{1,3},{6,4},{7,5},{8,10},{9,11},{14,12},{15,13},{16,18},{17,... | collective-permute-start | bytes 1179656 | tf_op jit(solution)/shard_map/ppermute | solution.py:25
  87.9 15.7 %collective-permute-start.31 = (bf16[2,64,2048]{2,1,0:T(8,128)(2,1)}, bf16[2,64,2048]{2,1,0:T(8,128)(2,1)}, u32[]{:S(2)}, u32[]{:S(2)}) collective-permute-start(bf16[2,64,2048]{2,1,0:T(8,128)(2,1)} %add_convert_fusion.1), channel_id=1, source_target_pairs={{2,4},{3,5},{4,2},{5,3},{10,12},{11,13},{12,10},{13,11},{18,20},{1... | collective-permute-start | bytes 1572872 | tf_op jit(solution)/shard_map/ppermute | solution.py:25
  89.3 9.2 %copy-start.19 = (f32[2,64,1536]{2,1,0:T(8,128)S(1)}, f32[2,64,1536]{2,1,0:T(8,128)}, u32[]{:S(2)}) copy-start(f32[2,64,1536]{2,1,0:T(8,128)} %copy-done.18) | copy-start | bytes 2359300
  89.3 10.1 %copy-start.14 = (f32[2,64,1536]{2,1,0:T(8,128)S(1)}, f32[2,64,1536]{2,1,0:T(8,128)}, u32[]{:S(2)}) copy-start(f32[2,64,1536]{2,1,0:T(8,128)} %copy-done.13) | copy-start | bytes 2359300
  97.0 9.2 %collective-permute-start.40 = (bf16[64,1536]{1,0:T(8,128)(2,1)}, bf16[64,1536]{1,0:T(8,128)(2,1)S(1)}, u32[]{:S(2)}, u32[]{:S(2)}) collective-permute-start(bf16[64,1536]{1,0:T(8,128)(2,1)} %shard_map.116), channel_id=1, source_target_pairs={{0,2},{1,3},{6,4},{7,5},{8,10},{9,11},{14,12},{15,13},{16,18},{17,... | collective-permute-start | bytes 589832 | tf_op jit(solution)/shard_map/ppermute | solution.py:25
  98.7 8.4 %collective-permute-start.23 = (bf16[2,64,1536]{2,1,0:T(8,128)(2,1)S(1)}, bf16[2,64,1536]{2,1,0:T(8,128)(2,1)S(1)}, u32[]{:S(2)}, u32[]{:S(2)}) collective-permute-start(bf16[2,64,1536]{2,1,0:T(8,128)(2,1)S(1)} %add_convert_fusion.4), channel_id=1, source_target_pairs={{2,4},{3,5},{4,2},{5,3},{10,12},{11,13},{12,10},{13,11},{18,20},{1... | collective-permute-start | bytes 1179656 | tf_op jit(solution)/shard_map/ppermute | solution.py:25
  99.4 7.7 %copy-start.10 = (f32[2,64,1536]{2,1,0:T(8,128)S(1)}, f32[2,64,1536]{2,1,0:T(8,128)}, u32[]{:S(2)}) copy-start(f32[2,64,1536]{2,1,0:T(8,128)} %copy-done.9) | copy-start | bytes 2359300
  100.6 10.9 %collective-permute-start.10 = (bf16[2,64,1536]{2,1,0:T(8,128)(2,1)S(1)}, bf16[2,64,1536]{2,1,0:T(8,128)(2,1)S(1)}, u32[]{:S(2)}, u32[]{:S(2)}) collective-permute-start(bf16[2,64,1536]{2,1,0:T(8,128)(2,1)S(1)} %fusion.5), channel_id=1, source_target_pairs={{0,2},{1,3},{6,4},{7,5},{8,10},{9,11},{14,12},{15,13},{16,18},{17,... | collective-permute-start | bytes 1179656 | tf_op jit(solution)/shard_map/ppermute | solution.py:25
  105.0 27.6 %collective-permute-start.32 = (bf16[2,64,2048]{2,1,0:T(8,128)(2,1)S(1)}, bf16[2,64,2048]{2,1,0:T(8,128)(2,1)}, u32[]{:S(2)}, u32[]{:S(2)}) collective-permute-start(bf16[2,64,2048]{2,1,0:T(8,128)(2,1)S(1)} %add_convert_fusion), channel_id=1, source_target_pairs={{4,6},{5,7},{2,0},{3,1},{12,14},{13,15},{10,8},{11,9},{20,22},{21,... | collective-permute-start | bytes 1572872 | tf_op jit(solution)/shard_map/ppermute | solution.py:25
  106.3 73.0 %collective-permute-start.44 = (bf16[64,1536]{1,0:T(8,128)(2,1)S(1)}, bf16[64,1536]{1,0:T(8,128)(2,1)S(1)}, u32[]{:S(2)}, u32[]{:S(2)}) collective-permute-start(bf16[64,1536]{1,0:T(8,128)(2,1)S(1)} %broadcast_select_fusion.2.refs_1_), channel_id=1, source_target_pairs={{0,1},{1,0},{2,3},{3,2},{4,5},{5,4},{6,7},{7,6},{8,9},{9,8},{10,11... | collective-permute-start | bytes 589832 | tf_op jit(solution)/shard_map/ppermute | solution.py:19
  106.4 2.9 %collective-permute-start.41 = (bf16[64,1536]{1,0:T(8,128)(2,1)S(1)}, bf16[64,1536]{1,0:T(8,128)(2,1)S(1)}, u32[]{:S(2)}, u32[]{:S(2)}) collective-permute-start(bf16[64,1536]{1,0:T(8,128)(2,1)S(1)} %collective-permute-done.40), channel_id=1, source_target_pairs={{2,4},{3,5},{4,2},{5,3},{10,12},{11,13},{12,10},{13,11},{18,20},{1... | collective-permute-start | bytes 589832 | tf_op jit(solution)/shard_map/ppermute | solution.py:25
  108.0 32.5 %collective-permute-start.24 = (bf16[2,64,1536]{2,1,0:T(8,128)(2,1)}, bf16[2,64,1536]{2,1,0:T(8,128)(2,1)S(1)}, u32[]{:S(2)}, u32[]{:S(2)}) collective-permute-start(bf16[2,64,1536]{2,1,0:T(8,128)(2,1)} %add_convert_fusion.3), channel_id=1, source_target_pairs={{4,6},{5,7},{2,0},{3,1},{12,14},{13,15},{10,8},{11,9},{20,22},{21,... | collective-permute-start | bytes 1179656 | tf_op jit(solution)/shard_map/ppermute | solution.py:25
  109.3 23.2 %collective-permute-start.42 = (bf16[64,1536]{1,0:T(8,128)(2,1)S(1)}, bf16[64,1536]{1,0:T(8,128)(2,1)S(1)}, u32[]{:S(2)}, u32[]{:S(2)}) collective-permute-start(bf16[64,1536]{1,0:T(8,128)(2,1)S(1)} %collective-permute-done.41), channel_id=1, source_target_pairs={{4,6},{5,7},{2,0},{3,1},{12,14},{13,15},{10,8},{11,9},{20,22},{21,... | collective-permute-start | bytes 589832 | tf_op jit(solution)/shard_map/ppermute | solution.py:25
  112.6 35.1 %collective-permute-start.11 = (bf16[2,64,1536]{2,1,0:T(8,128)(2,1)S(1)}, bf16[2,64,1536]{2,1,0:T(8,128)(2,1)S(1)}, u32[]{:S(2)}, u32[]{:S(2)}) collective-permute-start(bf16[2,64,1536]{2,1,0:T(8,128)(2,1)S(1)} %add_convert_fusion.6), channel_id=1, source_target_pairs={{2,4},{3,5},{4,2},{5,3},{10,12},{11,13},{12,10},{13,11},{18,20},{1... | collective-permute-start | bytes 1179656 | tf_op jit(solution)/shard_map/ppermute | solution.py:25
  132.5 15.2 %copy-start.8 = (f32[2,64,1536]{2,1,0:T(8,128)S(1)}, f32[2,64,1536]{2,1,0:T(8,128)}, u32[]{:S(2)}) copy-start(f32[2,64,1536]{2,1,0:T(8,128)} %copy-done.7) | copy-start | bytes 2359300
  132.5 46.9 %collective-permute-start.43 = (bf16[64,1536]{1,0:T(8,128)(2,1)S(1)}, bf16[64,1536]{1,0:T(8,128)(2,1)S(1)}, u32[]{:S(2)}, u32[]{:S(2)}) collective-permute-start(bf16[64,1536]{1,0:T(8,128)(2,1)S(1)} %broadcast_select_fusion.5.refs_0_), channel_id=1, source_target_pairs={{0,1},{1,0},{2,3},{3,2},{4,5},{5,4},{6,7},{7,6},{8,9},{9,8},{10,11... | collective-permute-start | bytes 589832 | tf_op jit(solution)/shard_map/ppermute | solution.py:19
  138.2 11.9 %copy-start.26 = (bf16[64,2048]{1,0:T(8,128)(2,1)S(1)}, bf16[64,2048]{1,0:T(8,128)(2,1)}, u32[]{:S(2)}) copy-start(bf16[64,2048]{1,0:T(8,128)(2,1)} %shard_map.115) | copy-start | bytes 786436
  138.2 11.9 %collective-permute-start.33 = (bf16[64,2048]{1,0:T(8,128)(2,1)}, bf16[64,2048]{1,0:T(8,128)(2,1)}, u32[]{:S(2)}, u32[]{:S(2)}) collective-permute-start(bf16[64,2048]{1,0:T(8,128)(2,1)} %shard_map.115), channel_id=1, source_target_pairs={{0,2},{1,3},{6,4},{7,5},{8,10},{9,11},{14,12},{15,13},{16,18},{17,... | collective-permute-start | bytes 786440 | tf_op jit(solution)/shard_map/ppermute | solution.py:25
  145.7 6.5 %collective-permute-start.25 = (bf16[64,1536]{1,0:T(8,128)(2,1)}, bf16[64,1536]{1,0:T(8,128)(2,1)}, u32[]{:S(2)}, u32[]{:S(2)}) collective-permute-start(bf16[64,1536]{1,0:T(8,128)(2,1)} %shard_map.114), channel_id=1, source_target_pairs={{0,2},{1,3},{6,4},{7,5},{8,10},{9,11},{14,12},{15,13},{16,18},{17,... | collective-permute-start | bytes 589832 | tf_op jit(solution)/shard_map/ppermute | solution.py:25
  147.7 21.0 %copy-start.28 = (bf16[64,1536]{1,0:T(8,128)(2,1)S(1)}, bf16[64,1536]{1,0:T(8,128)(2,1)}, u32[]{:S(2)}) copy-start(bf16[64,1536]{1,0:T(8,128)(2,1)} %shard_map.114) | copy-start | bytes 589828
  148.8 13.2 %collective-permute-start.12 = (bf16[2,64,1536]{2,1,0:T(8,128)(2,1)S(1)}, bf16[2,64,1536]{2,1,0:T(8,128)(2,1)S(1)}, u32[]{:S(2)}, u32[]{:S(2)}) collective-permute-start(bf16[2,64,1536]{2,1,0:T(8,128)(2,1)S(1)} %add_convert_fusion.5), channel_id=1, source_target_pairs={{4,6},{5,7},{2,0},{3,1},{12,14},{13,15},{10,8},{11,9},{20,22},{21,... | collective-permute-start | bytes 1179656 | tf_op jit(solution)/shard_map/ppermute | solution.py:25
  150.2 18.6 %collective-permute-start.34 = (bf16[64,2048]{1,0:T(8,128)(2,1)}, bf16[64,2048]{1,0:T(8,128)(2,1)S(1)}, u32[]{:S(2)}, u32[]{:S(2)}) collective-permute-start(bf16[64,2048]{1,0:T(8,128)(2,1)} %collective-permute-done.33), channel_id=1, source_target_pairs={{2,4},{3,5},{4,2},{5,3},{10,12},{11,13},{12,10},{13,11},{18,20},{1... | collective-permute-start | bytes 786440 | tf_op jit(solution)/shard_map/ppermute | solution.py:25
  152.1 16.6 %collective-permute-start.26 = (bf16[64,1536]{1,0:T(8,128)(2,1)}, bf16[64,1536]{1,0:T(8,128)(2,1)S(1)}, u32[]{:S(2)}, u32[]{:S(2)}) collective-permute-start(bf16[64,1536]{1,0:T(8,128)(2,1)} %collective-permute-done.25), channel_id=1, source_target_pairs={{2,4},{3,5},{4,2},{5,3},{10,12},{11,13},{12,10},{13,11},{18,20},{1... | collective-permute-start | bytes 589832 | tf_op jit(solution)/shard_map/ppermute | solution.py:25
  167.2 5.6 %collective-permute-start.16 = (bf16[64,1536]{1,0:T(8,128)(2,1)}, bf16[64,1536]{1,0:T(8,128)(2,1)S(1)}, u32[]{:S(2)}, u32[]{:S(2)}) collective-permute-start(bf16[64,1536]{1,0:T(8,128)(2,1)} %shard_map.112), channel_id=1, source_target_pairs={{0,2},{1,3},{6,4},{7,5},{8,10},{9,11},{14,12},{15,13},{16,18},{17,... | collective-permute-start | bytes 589832 | tf_op jit(solution)/shard_map/ppermute | solution.py:25
  168.7 25.5 %collective-permute-start.37 = (bf16[64,2048]{1,0:T(8,128)(2,1)S(1)}, bf16[64,2048]{1,0:T(8,128)(2,1)S(1)}, u32[]{:S(2)}, u32[]{:S(2)}) collective-permute-start(bf16[64,2048]{1,0:T(8,128)(2,1)S(1)} %broadcast_select_fusion.refs_1_), channel_id=1, source_target_pairs={{0,1},{1,0},{2,3},{3,2},{4,5},{5,4},{6,7},{7,6},{8,9},{9,8},{10,11... | collective-permute-start | bytes 786440 | tf_op jit(solution)/shard_map/ppermute | solution.py:19
  168.8 9.6 %collective-permute-start.27 = (bf16[64,1536]{1,0:T(8,128)(2,1)S(1)}, bf16[64,1536]{1,0:T(8,128)(2,1)S(1)}, u32[]{:S(2)}, u32[]{:S(2)}) collective-permute-start(bf16[64,1536]{1,0:T(8,128)(2,1)S(1)} %collective-permute-done.26.refs_5_), channel_id=1, source_target_pairs={{4,6},{5,7},{2,0},{3,1},{12,14},{13,15},{10,8},{11,9},{20,22},{21,... | collective-permute-start | bytes 589832 | tf_op jit(solution)/shard_map/ppermute | solution.py:25
  172.9 12.0 %collective-permute-start.35 = (bf16[64,2048]{1,0:T(8,128)(2,1)S(1)}, bf16[64,2048]{1,0:T(8,128)(2,1)S(1)}, u32[]{:S(2)}, u32[]{:S(2)}) collective-permute-start(bf16[64,2048]{1,0:T(8,128)(2,1)S(1)} %collective-permute-done.34), channel_id=1, source_target_pairs={{4,6},{5,7},{2,0},{3,1},{12,14},{13,15},{10,8},{11,9},{20,22},{21,... | collective-permute-start | bytes 786440 | tf_op jit(solution)/shard_map/ppermute | solution.py:25
  178.4 6.6 %collective-permute-start.17 = (bf16[64,1536]{1,0:T(8,128)(2,1)S(1)}, bf16[64,1536]{1,0:T(8,128)(2,1)S(1)}, u32[]{:S(2)}, u32[]{:S(2)}) collective-permute-start(bf16[64,1536]{1,0:T(8,128)(2,1)S(1)} %collective-permute-done.16.refs_6_), channel_id=1, source_target_pairs={{2,4},{3,5},{4,2},{5,3},{10,12},{11,13},{12,10},{13,11},{18,20},{1... | collective-permute-start | bytes 589832 | tf_op jit(solution)/shard_map/ppermute | solution.py:25
  179.3 22.7 %collective-permute-start.29 = (bf16[64,1536]{1,0:T(8,128)(2,1)S(1)}, bf16[64,1536]{1,0:T(8,128)(2,1)S(1)}, u32[]{:S(2)}, u32[]{:S(2)}) collective-permute-start(bf16[64,1536]{1,0:T(8,128)(2,1)S(1)} %broadcast_select_fusion.3.refs_1_), channel_id=1, source_target_pairs={{0,1},{1,0},{2,3},{3,2},{4,5},{5,4},{6,7},{7,6},{8,9},{9,8},{10,11... | collective-permute-start | bytes 589832 | tf_op jit(solution)/shard_map/ppermute | solution.py:19
  179.4 22.6 %collective-permute-start.28 = (bf16[64,1536]{1,0:T(8,128)(2,1)S(1)}, bf16[64,1536]{1,0:T(8,128)(2,1)S(1)}, u32[]{:S(2)}, u32[]{:S(2)}) collective-permute-start(bf16[64,1536]{1,0:T(8,128)(2,1)S(1)} %broadcast_select_fusion.6.refs_0_), channel_id=1, source_target_pairs={{0,1},{1,0},{2,3},{3,2},{4,5},{5,4},{6,7},{7,6},{8,9},{9,8},{10,11... | collective-permute-start | bytes 589832 | tf_op jit(solution)/shard_map/ppermute | solution.py:19
  184.9 22.3 %collective-permute-start.20 = (bf16[64,1536]{1,0:T(8,128)(2,1)S(1)}, bf16[64,1536]{1,0:T(8,128)(2,1)S(1)}, u32[]{:S(2)}, u32[]{:S(2)}) collective-permute-start(bf16[64,1536]{1,0:T(8,128)(2,1)S(1)} %broadcast_select_fusion.4.refs_1_), channel_id=1, source_target_pairs={{0,1},{1,0},{2,3},{3,2},{4,5},{5,4},{6,7},{7,6},{8,9},{9,8},{10,11... | collective-permute-start | bytes 589832 | tf_op jit(solution)/shard_map/ppermute | solution.py:19
  185.0 9.1 %collective-permute-start.18 = (bf16[64,1536]{1,0:T(8,128)(2,1)S(1)}, bf16[64,1536]{1,0:T(8,128)(2,1)S(1)}, u32[]{:S(2)}, u32[]{:S(2)}) collective-permute-start(bf16[64,1536]{1,0:T(8,128)(2,1)S(1)} %collective-permute-done.17.refs_6_), channel_id=1, source_target_pairs={{4,6},{5,7},{2,0},{3,1},{12,14},{13,15},{10,8},{11,9},{20,22},{21,... | collective-permute-start | bytes 589832 | tf_op jit(solution)/shard_map/ppermute | solution.py:25
  194.2 1.5 collective-permute-start.36
  194.2 13.0 %collective-permute-start.19 = (bf16[64,1536]{1,0:T(8,128)(2,1)S(1)}, bf16[64,1536]{1,0:T(8,128)(2,1)S(1)}, u32[]{:S(2)}, u32[]{:S(2)}) collective-permute-start(bf16[64,1536]{1,0:T(8,128)(2,1)S(1)} %broadcast_select_fusion.7.refs_0_), channel_id=1, source_target_pairs={{0,1},{1,0},{2,3},{3,2},{4,5},{5,4},{6,7},{7,6},{8,9},{9,8},{10,11... | collective-permute-start | bytes 589832 | tf_op jit(solution)/shard_map/ppermute | solution.py:19
  207.2 23.8 %copy-start.24 = (f32[64,16,128]{2,1,0:T(8,128)S(1)}, f32[64,16,128]{2,1,0:T(8,128)}, u32[]{:S(2)}) copy-start(f32[64,16,128]{2,1,0:T(8,128)} %copy-done.23) | copy-start | bytes 1572868
  212.5 20.9 %copy-start.1 = (bf16[64,16384]{1,0:T(8,128)(2,1)S(1)}, bf16[64,16384]{1,0:T(8,128)(2,1)}, u32[]{:S(2)}) copy-start(bf16[64,16384]{1,0:T(8,128)(2,1)} %param.12) | copy-start | bytes 6291460
  214.6 9.5 %collective-permute-start.45 = (bf16[64,2048]{1,0:T(8,128)(2,1)}, bf16[64,2048]{1,0:T(8,128)(2,1)}, u32[]{:S(2)}, u32[]{:S(2)}) collective-permute-start(bf16[64,2048]{1,0:T(8,128)(2,1)} %get-tuple-element.44), channel_id=1, source_target_pairs={{0,8},{8,0},{16,24},{24,16},{1,9},{9,1},{17,25},{25,17},{2,10},{10... | collective-permute-start | bytes 786440 | tf_op jit(solution)/shard_map/ppermute | solution.py:19
  216.1 13.8 %collective-permute-start.47 = (bf16[64,2048]{1,0:T(8,128)(2,1)S(1)}, bf16[64,2048]{1,0:T(8,128)(2,1)}, u32[]{:S(2)}, u32[]{:S(2)}) collective-permute-start(bf16[64,2048]{1,0:T(8,128)(2,1)S(1)} %get-tuple-element.45), channel_id=1, source_target_pairs={{0,24},{8,16},{16,8},{24,0},{1,25},{9,17},{17,9},{25,1},{2,26},{10... | collective-permute-start | bytes 786440 | tf_op jit(solution)/shard_map/ppermute | solution.py:19
  217.5 13.5 %collective-permute-start.46 = (bf16[64,2048]{1,0:T(8,128)(2,1)S(1)}, bf16[64,2048]{1,0:T(8,128)(2,1)}, u32[]{:S(2)}, u32[]{:S(2)}) collective-permute-start(bf16[64,2048]{1,0:T(8,128)(2,1)S(1)} %get-tuple-element.46), channel_id=1, source_target_pairs={{0,16},{8,24},{16,0},{24,8},{1,17},{9,25},{17,1},{25,9},{2,18},{10... | collective-permute-start | bytes 786440 | tf_op jit(solution)/shard_map/ppermute | solution.py:19
  (18 other events, 47.0 us)
